TPU v7x, 128 devices: a whole 4x4x4 slice. The times are simulated.
128 devices in a mesh: dp: 16 (over y_hi, x, core), row: 2 (over y_lo), col: 4 (over z).
Axes of the slice: x: 4, y: 4 (y_hi: 2, y_lo: 2; y = y_hi * 2 + y_lo), z: 4, core: 2. Of those that a mesh axis runs over, the one named last changes fastest.
Arguments:
- tokens: bfloat16 [16384, 1024], P(('dp', 'col'), 'row'), may hold values from -6 to 6
- mixer_gain: float32 [1024], P('row'), may hold values from 0.25 to 1.75
- in_weight: bfloat16 [3, 1024, 1024], P(None, 'row', 'col'), may hold values from -0.1875 to 0.1875
- conv_kernel: float32 [3, 1024], P(None, 'col'), may hold values from -1 to 1
- out_weight: bfloat16 [1024, 1024], P('col', 'row'), may hold values from -0.1875 to 0.1875
- ffn_gain: float32 [1024], P('row'), may hold values from 0.25 to 1.75
- gate_up_weight: bfloat16 [2, 1024, 4608], P(None, 'row', 'col'), may hold values from -0.1875 to 0.1875
- down_weight: bfloat16 [4608, 1024], P('col', 'row'), may hold values from -0.09375 to 0.09375
- conv_reach: int32 [16384], P(('dp', 'row')), may hold values from 0 to 2, as said below
- cotangent: bfloat16 [16384, 1024], P(('dp', 'col'), 'row'), may hold values from -6 to 6
Outputs:
- mixed: bfloat16 [16384, 1024], P(('dp', 'col'), 'row')
- grad_tokens: float32 [16384, 1024], P(('dp', 'col'), 'row')
- grad_mixer_gain: float32 [1024], P('row')
- grad_in_weight: float32 [3, 1024, 1024], P(None, 'row', 'col')
- grad_conv_kernel: float32 [3, 1024], P(None, 'col')
- grad_out_weight: float32 [1024, 1024], P('col', 'row')
- grad_ffn_gain: float32 [1024], P('row')
- grad_gate_up_weight: float32 [2, 1024, 4608], P(None, 'row', 'col')
- grad_down_weight: float32 [4608, 1024], P('col', 'row')
Inputs may be any that keep to these rules, and one draw needn't show every extreme that they name: `conv_reach`: the first token of every sequence of 1024 tokens begins a document.
All inputs are finite; a program needn't handle non-finite values.
Results may differ from a plain program's by a relative error of at most 0.028.
Values may be sent and summed in bfloat16 or wider, within the bound.
A program may use at most 128 MiB of HBM per device.

v0:
```python
import jax
import jax.numpy as jnp
from jax import lax
from jax.sharding import PartitionSpec as P

D = 1024


norm_eps = 1e-05


def joined_along(tiles, dim):
    lengths = list(tiles.shape[1:])
    lengths[dim] *= tiles.shape[0]
    return jnp.moveaxis(tiles, 0, dim).reshape(lengths)


def from_everyone(value, axis):
    copies = jnp.broadcast_to(value, (lax.axis_size(axis), *value.shape))
    return lax.all_to_all(copies, axis, split_axis=0, concat_axis=0, tiled=True)


def gathered_copies(value, axis, dim):
    return joined_along(from_everyone(value, axis), dim)


def cut_along(value, dim, count):
    before, after = (value.shape[:dim], value.shape[dim + 1 :])
    return jnp.moveaxis(value.reshape(*before, count, -1, *after), dim, 0)


def sent_and_summed(value, axis, dim):
    tiles = cut_along(value, dim, lax.axis_size(axis))
    arrived = lax.all_to_all(tiles, axis, split_axis=0, concat_axis=0, tiled=True)
    return arrived.astype(jnp.float32).sum(axis=0)


def over_copies(value, axis):
    return from_everyone(value, axis).sum(axis=0)


def from_behind(block, axis, distance):
    devices = range(lax.axis_size(axis))
    route = [(i - distance, i) for i in devices if i - distance in devices]
    return lax.ppermute(block, axis, route)


def packed_total(arrays, axis):
    vector, at, outs = (jnp.concatenate([a.reshape(-1) for a in arrays]), 0, [])
    total = over_copies(vector, axis)
    for a in arrays:
        outs.append(total[at : at + a.size].reshape(a.shape))
        at += a.size
    return tuple(outs)


def gather_columns(value):
    return gathered_copies(value, "col", 0)


def gather_rows(value):
    return lax.all_gather(value, "row", axis=0, tiled=True)


def scatter_rows(gathered, product):
    count = gathered.shape[0] // lax.axis_size("row")

    def term(start, length):
        return product(gathered)

    return sent_and_summed(
        term(jnp.int32(0), count * lax.axis_size("row")).astype(jnp.bfloat16), "row", 0
    )


def scatter_columns(gathered, product):
    count = gathered.shape[0] // lax.axis_size("col")

    def term(start, length):
        return product(gathered)

    return sent_and_summed(
        term(jnp.int32(0), count * lax.axis_size("col")).astype(jnp.bfloat16), "col", 0
    )


def row_total(value):
    return over_copies(value, "row")


def norm_forward(value, gain):
    total = row_total(jnp.sum(value * value, axis=1))
    scale = lax.rsqrt(total / D + norm_eps)[:, None]
    return (scale, (value * scale * gain).astype(jnp.bfloat16))


def norm_backward(value, scale, gain, grad_normed):
    weighted = grad_normed * gain
    inner = row_total(jnp.sum(weighted * value, axis=1))[:, None]
    grad_value = scale * weighted - value * (scale * scale * scale) * inner / D
    grad_gain = jnp.sum(grad_normed * value * scale, axis=0)
    return (grad_value, grad_gain)


def project_in(rows, weight):
    result = jnp.einsum("td,kdf->tkf", rows, weight, preferred_element_type=jnp.float32)
    return result.reshape(rows.shape[0], -1)


def project_back(rows, weight):
    parts = rows.reshape(rows.shape[0], weight.shape[0], weight.shape[2])
    return jnp.einsum("tkf,kdf->td", parts, weight, preferred_element_type=jnp.float32)


def project_out(rows, weight):
    return jnp.dot(rows, weight, preferred_element_type=jnp.float32)


def project_out_back(rows, weight):
    return jnp.einsum("td,fd->tf", rows, weight, preferred_element_type=jnp.float32)


def swiglu(gate, up):
    return jax.nn.silu(gate) * up


def per_device(
    tokens,
    mixer_gain,
    in_weight,
    conv_kernel,
    out_weight,
    ffn_gain,
    gate_up_weight,
    down_weight,
    conv_reach,
    cotangent,
):
    inputs = tokens.astype(jnp.float32)
    scale_one, normed_one = norm_forward(inputs, mixer_gain)
    gathered_one = gather_columns(normed_one)
    mixed_in = scatter_rows(gathered_one, lambda rows: project_in(rows, in_weight))
    length = mixed_in.shape[0]
    width = in_weight.shape[2]
    hid_width = gate_up_weight.shape[2]
    mixed_in = mixed_in.reshape(length, 3, width)
    gate_b = mixed_in[:, 0]
    gate_c = mixed_in[:, 1]
    values = mixed_in[:, 2]
    product = gate_b * values
    earlier = from_behind(product[length - 2 :], "row", 1)
    extended = jnp.concatenate([earlier, product], axis=0)
    masks = [(conv_reach >= offset).astype(jnp.float32)[:, None] for offset in (1, 2)]
    conv_out = conv_kernel[0] * product
    conv_out = conv_out + conv_kernel[1] * extended[1 : length + 1] * masks[0]
    conv_out = conv_out + conv_kernel[2] * extended[0:length] * masks[1]
    gated = (gate_c * conv_out).astype(jnp.bfloat16)
    gathered_gated = gather_rows(gated)
    branch = scatter_columns(gathered_gated, lambda rows: project_out(rows, out_weight))
    hidden = inputs + branch
    scale_two, normed_two = norm_forward(hidden, ffn_gain)
    gathered_two = gather_columns(normed_two)
    own_half = lax.all_to_all(gathered_two, "row", split_axis=0, concat_axis=1, tiled=True)
    gate_up = jnp.einsum(
        "td,kdf->tkf",
        own_half,
        lax.all_gather(gate_up_weight, "row", axis=1, tiled=True),
        preferred_element_type=jnp.float32,
    )
    gate = gate_up[:, 0]
    up = gate_up[:, 1]
    active = swiglu(gate, up).astype(jnp.bfloat16)
    gathered_active = gather_rows(active)
    ffn_out = scatter_columns(gathered_active, lambda rows: project_out(rows, down_weight))
    mixed = (hidden + ffn_out).astype(jnp.bfloat16)
    grad_out = cotangent.astype(jnp.float32)
    gathered_grad = gather_columns(cotangent)
    grad_down = jnp.einsum(
        "tf,td->fd", gathered_active, gathered_grad, preferred_element_type=jnp.float32
    )
    grad_active = scatter_rows(gathered_grad, lambda rows: project_out_back(rows, down_weight))
    unused, pullback = jax.vjp(swiglu, gate, up)
    grad_gate, grad_up = pullback(grad_active)
    grad_gate_up = jnp.stack([grad_gate, grad_up], axis=1).astype(jnp.bfloat16).reshape(length, -1)
    gathered_gate_up = gather_rows(grad_gate_up)
    grad_gate_up_weight = jnp.einsum(
        "td,tkf->kdf",
        gathered_two,
        gathered_gate_up.reshape(-1, 2, hid_width),
        preferred_element_type=jnp.float32,
    )
    grad_normed_two = scatter_columns(
        gathered_gate_up, lambda rows: project_back(rows, gate_up_weight)
    )
    grad_hidden_norm, grad_ffn_gain = norm_backward(hidden, scale_two, ffn_gain, grad_normed_two)
    grad_hidden = grad_out + grad_hidden_norm
    grad_branch = grad_hidden.astype(jnp.bfloat16)
    gathered_branch = gather_columns(grad_branch)
    grad_out_weight = jnp.einsum(
        "tc,td->cd", gathered_gated, gathered_branch, preferred_element_type=jnp.float32
    )
    grad_gated = scatter_rows(gathered_branch, lambda rows: project_out_back(rows, out_weight))
    grad_c = grad_gated * conv_out
    grad_conv = grad_gated * gate_c
    first_masked = grad_conv * masks[0]
    second_masked = grad_conv * masks[1]
    later = from_behind(jnp.stack([first_masked[:2], second_masked[:2]], axis=0), "row", -1)
    first_ext = jnp.concatenate([first_masked, later[0]], axis=0)
    second_ext = jnp.concatenate([second_masked, later[1]], axis=0)
    grad_product = (
        conv_kernel[0] * grad_conv
        + conv_kernel[1] * first_ext[1 : length + 1]
        + conv_kernel[2] * second_ext[2 : length + 2]
    )
    grad_kernel = jnp.stack(
        [
            jnp.sum(grad_conv * product, axis=0),
            jnp.sum(first_masked * extended[1 : length + 1], axis=0),
            jnp.sum(second_masked * extended[0:length], axis=0),
        ],
        axis=0,
    )
    grad_mixed = jnp.stack([grad_product * values, grad_c, grad_product * gate_b], axis=1).astype(
        jnp.bfloat16
    )
    gathered_mixed = gather_rows(grad_mixed.reshape(length, -1))
    grad_in_weight = jnp.einsum(
        "td,tkf->kdf",
        gathered_one,
        gathered_mixed.reshape(-1, 3, width),
        preferred_element_type=jnp.float32,
    )
    grad_normed_one = scatter_columns(gathered_mixed, lambda rows: project_back(rows, in_weight))
    grad_inputs_norm, grad_mixer_gain = norm_backward(
        inputs, scale_one, mixer_gain, grad_normed_one
    )
    grad_tokens = grad_hidden + grad_inputs_norm
    grad_in_weight, grad_out_weight, grad_gate_up_weight, grad_down = (
        lax.psum(grad_in_weight.astype(jnp.bfloat16), "dp").astype(jnp.float32),
        lax.psum(grad_out_weight.astype(jnp.bfloat16), "dp").astype(jnp.float32),
        lax.psum(grad_gate_up_weight.astype(jnp.bfloat16), "dp").astype(jnp.float32),
        lax.psum(grad_down.astype(jnp.bfloat16), "dp").astype(jnp.float32),
    )
    grad_kernel = over_copies(grad_kernel, ("dp", "row"))
    grad_mixer_gain, grad_ffn_gain = packed_total((grad_mixer_gain, grad_ffn_gain), ("dp", "col"))
    return (
        mixed,
        grad_tokens,
        grad_mixer_gain,
        grad_in_weight,
        grad_kernel,
        grad_out_weight,
        grad_ffn_gain,
        grad_gate_up_weight,
        grad_down,
    )


def solution(mesh):
    return jax.shard_map(
        per_device,
        mesh=mesh,
        in_specs=(
            P(("dp", "col"), "row"),
            P("row"),
            P(None, "row", "col"),
            P(None, "col"),
            P("col", "row"),
            P("row"),
            P(None, "row", "col"),
            P("col", "row"),
            P(("dp", "row")),
            P(("dp", "col"), "row"),
        ),
        out_specs=(
            P(("dp", "col"), "row"),
            P(("dp", "col"), "row"),
            P("row"),
            P(None, "row", "col"),
            P(None, "col"),
            P("col", "row"),
            P("row"),
            P(None, "row", "col"),
            P("col", "row"),
        ),
        check_vma=False,
    )
```

profile of v0, /device:TPU:1, one launch (start us, length us, event | category | flops | bytes accessed | tf_op | source)
XLA Modules:
  0.0 571.9 jit_solution(7158761277564637482)
XLA Ops:
  8.4 5.8 %all_to_all.109 = f32[2,1,256]{2,1,0:T(1,128)S(1)} all-to-all(f32[2,1,256]{2,1,0:T(1,128)S(1)} %broadcast_in_dim.40), channel_id=1, replica_groups=mesh['dp'=16,'row'=2,'col'=4] {'row'}, dimensions={0} | all-to-all | bytes 4096 | tf_op jit(solution)/shard_map/all_to_all | solution.py:20
  17.0 5.0 all-to-all-start.1
  23.2 11.3 %all-to-all-done.1 = bf16[4,256,512]{2,1,0:T(8,128)(2,1)S(1)} async-done(((bf16[4,256,512]{2,1,0:T(8,128)(2,1)}), bf16[4,256,512]{2,1,0:T(8,128)(2,1)S(1)}, u32[]{:S(2)}, u32[]{:S(2)}) %all-to-all-start.1) | async-done | bytes 1048608 | tf_op jit(solution)/shard_map/all_to_all | solution.py:20
  34.5 3.7 convolution_convert_fusion.3
  38.1 3.8 all-to-all-start.2
  43.3 14.3 %all-to-all-done.2 = bf16[2,512,768]{2,1,0:T(8,128)(2,1)S(1)} async-done(((bf16[2,512,768]{2,1,0:T(8,128)(2,1)}), bf16[2,512,768]{2,1,0:T(8,128)(2,1)S(1)}, u32[]{:S(2)}, u32[]{:S(2)}) %all-to-all-start.2) | async-done | bytes 1572896 | tf_op jit(solution)/shard_map/all_to_all | solution.py:34
  57.6 1.4 convert_reduce_fusion.1
  59.0 2.1 copy.58
  62.2 1.3 copy.83
  63.5 1.5 copy.84
  65.6 2.8 collective-permute-start
  69.4 1.8 fusion.27
  71.2 13.2 %all_gather.15 = bf16[1024,256]{1,0:T(8,128)(2,1)S(1)} all-gather(bf16[512,256]{1,0:T(8,128)(2,1)S(1)} %get-tuple-element.74), channel_id=1, replica_groups=mesh['dp'=16,'row'=2,'col'=4] {'row'}, dimensions={0}, use_global_device_ids=true | all-gather | bytes 786432 | tf_op jit(solution)/shard_map/all_gather | solution.py:62
  85.2 12.9 %all_to_all.110 = bf16[4,256,512]{2,1,0:T(8,128)(2,1)} all-to-all(bf16[4,256,512]{2,1,0:T(8,128)(2,1)S(1)} %bitcast.125), channel_id=1, replica_groups=mesh['dp'=16,'row'=2,'col'=4] {'col'}, dimensions={0} | all-to-all | bytes 2097152 | tf_op jit(solution)/shard_map/all_to_all | solution.py:34
  99.1 3.6 all-to-all-start.8
  103.8 8.7 %all-to-all-done.8 = bf16[4,256,512]{2,1,0:T(8,128)(2,1)S(1)} async-done(((bf16[4,256,512]{2,1,0:T(8,128)(2,1)}), bf16[4,256,512]{2,1,0:T(8,128)(2,1)S(1)}, u32[]{:S(2)}, u32[]{:S(2)}) %all-to-all-start.8) | async-done | bytes 1048608 | tf_op jit(solution)/shard_map/all_to_all | solution.py:20
  113.1 3.2 all-to-all-start.4
  116.3 3.0 convolution_convert_fusion
  119.9 3.9 all-to-all-start.9
  123.8 1.3 reduce_sum.205
  125.1 1.2 multiply_multiply_fusion.1
  126.9 1.9 multiply_convert_fusion.1
  128.7 14.3 %all-to-all-done.9 = bf16[2,512,1152]{2,1,0:T(8,128)(2,1)S(1)} async-done(((bf16[2,512,1152]{2,1,0:T(8,128)(2,1)}), bf16[2,512,1152]{2,1,0:T(8,128)(2,1)S(1)}, u32[]{:S(2)}, u32[]{:S(2)}) %all-to-all-start.9) | async-done | bytes 2359328 | tf_op jit(solution)/shard_map/all_to_all | solution.py:34
  144.0 12.9 %all_to_all.111 = bf16[4,256,512]{2,1,0:T(8,128)(2,1)} all-to-all(bf16[4,256,512]{2,1,0:T(8,128)(2,1)S(1)} %broadcast_in_dim.43), channel_id=1, replica_groups=mesh['dp'=16,'row'=2,'col'=4] {'col'}, dimensions={0} | all-to-all | bytes 2097152 | tf_op jit(solution)/shard_map/all_to_all | solution.py:20
  156.9 4.4 all-to-all-start.6
  161.6 1.8 convert_reduce_fusion
  163.4 6.3 %all-to-all-done.6 = bf16[2,512,512]{2,1,0:T(8,128)(2,1)} async-done(((bf16[2,512,512]{2,1,0:T(8,128)(2,1)}), bf16[2,512,512]{2,1,0:T(8,128)(2,1)}, u32[]{:S(2)}, u32[]{:S(2)}) %all-to-all-start.6) | async-done | bytes 1048608 | tf_op jit(solution)/shard_map/all_to_all | solution.py:163
  169.7 2.3 copy.63
  172.0 1.5 reshape.138
  173.6 5.4 fusion.36
  179.0 1.6 fusion.3
  181.4 2.5 copy.64
  184.0 4.2 fusion.5
  188.2 72.4 %all-gather.9.cloned.1.call-done = bf16[1024,2304]{0,1:T(8,128)(2,1)} async-done(((bf16[512,2304]{0,1:T(8,128)(2,1)}), bf16[1024,2304]{0,1:T(8,128)(2,1)}) %all-gather.9.cloned.1.call-update) | async-done | bytes 4718608 | tf_op jit(solution)/shard_map/all_gather | solution.py:62
  260.6 6.0 %bitcast_convert_fusion.1 = bf16[1024,512]{1,0:T(8,128)(2,1)} fusion(bf16[1024,2,1152]{0,2,1:T(8,128)(2,1)} %bitcast.149, bf16[2,512,1152]{2,1,0:T(8,128)(2,1)S(1)} %copy-done.18), kind=kOutput, calls=%fused_computation.23 | convolution fusion | flops 2416443392 | bytes 8126464 | tf_op jit(solution)/shard_map/tkf,kdf->td/dot_general | solution.py:112
  266.6 4.1 all-to-all-start.10
  270.7 31.7 %all-gather.7.cloned.1.call-done = bf16[1024,1152]{1,0:T(8,128)(2,1)} async-done(((bf16[512,1152]{1,0:T(8,128)(2,1)}), bf16[1024,1152]{1,0:T(8,128)(2,1)}) %all-gather.7.cloned.1.call-update) | async-done | bytes 2359312 | tf_op jit(solution)/shard_map/all_gather | solution.py:62
  302.5 4.1 convolution_convert_fusion.4
  306.6 4.3 all-to-all-start.7
  311.3 13.8 %all-to-all-done.7 = bf16[4,256,512]{2,1,0:T(8,128)(2,1)S(1)} async-done(((bf16[4,256,512]{2,1,0:T(8,128)(2,1)}), bf16[4,256,512]{2,1,0:T(8,128)(2,1)S(1)}, u32[]{:S(2)}, u32[]{:S(2)}) %all-to-all-start.7) | async-done | bytes 1048608 | tf_op jit(solution)/shard_map/all_to_all | solution.py:34
  325.7 3.2 all-to-all-start.11
  329.1 2.4 all-to-all-done.11
  332.5 14.5 %all_to_all.112 = bf16[4,256,512]{2,1,0:T(8,128)(2,1)S(1)} all-to-all(bf16[4,256,512]{2,1,0:T(8,128)(2,1)S(1)} %broadcast_in_dim.46), channel_id=1, replica_groups=mesh['dp'=16,'row'=2,'col'=4] {'col'}, dimensions={0} | all-to-all | bytes 2097152 | tf_op jit(solution)/shard_map/all_to_all | solution.py:20
  347.5 7.8 %all_to_all.113 = bf16[2,512,256]{2,1,0:T(8,128)(2,1)S(1)} all-to-all(bf16[2,512,256]{2,1,0:T(8,128)(2,1)S(1)} %bitcast.130), channel_id=1, replica_groups=mesh['dp'=16,'row'=2,'col'=4] {'row'}, dimensions={0} | all-to-all | bytes 1048576 | tf_op jit(solution)/shard_map/all_to_all | solution.py:34
  356.6 1.4 collective-permute-start.1
  358.0 3.1 collective-permute-done.1
  362.7 4.4 convolution_convert_fusion.2
  367.2 6.2 %fusion = bf16[2,512,1152]{1,2,0:T(8,128)(2,1)} fusion(bf16[1024,2,1152]{0,2,1:T(8,128)(2,1)} %bitcast.150, bf16[1024,512,1]{1,0,2:T(8,128)(2,1)S(1)} %bitcast.127), kind=kOutput, calls=%fused_computation.4 | convolution fusion | flops 2417098752 | bytes 8126464 | tf_op jit(solution)/shard_map/td,tkf->kdf/dot_general | solution.py:186
  374.6 22.5 %all-gather.11.cloned.1.call-done = bf16[1024,768]{0,1:T(8,128)(2,1)} async-done(((bf16[512,768]{0,1:T(8,128)(2,1)}), bf16[1024,768]{0,1:T(8,128)(2,1)}) %all-gather.11.cloned.1.call-update) | async-done | bytes 1572880 | tf_op jit(solution)/shard_map/all_gather | solution.py:62
  397.1 3.6 fusion.9
  401.4 7.2 %all-to-all-start.17 = ((f32[32,3,256]{2,1,0:T(4,128)}), f32[32,3,256]{2,1,0:T(4,128)S(1)}, u32[]{:S(2)}, u32[]{:S(2)}) async-start(f32[32,3,256]{2,1,0:T(4,128)} %broadcast_in_dim.49), calls=%async_computation.17 | async-start | bytes 262144 | tf_op jit(solution)/shard_map/all_to_all | solution.py:20
  408.7 3.4 bitcast_convert_fusion
  412.1 4.2 all-to-all-done.17
  416.2 4.3 all-to-all-start.14
  421.1 13.3 %all-to-all-done.14 = bf16[4,256,512]{2,1,0:T(8,128)(2,1)S(1)} async-done(((bf16[4,256,512]{2,1,0:T(8,128)(2,1)}), bf16[4,256,512]{2,1,0:T(8,128)(2,1)S(1)}, u32[]{:S(2)}, u32[]{:S(2)}) %all-to-all-start.14) | async-done | bytes 1048608 | tf_op jit(solution)/shard_map/all_to_all | solution.py:34
  435.4 3.2 all-to-all-start.15
  438.7 2.6 all-to-all-done.15
  442.1 7.3 %all-to-all-start.16 = ((f32[64,1,1024]{2,1,0:T(1,128)}), f32[64,1,1024]{2,1,0:T(1,128)S(1)}, u32[]{:S(2)}, u32[]{:S(2)}) async-start(f32[64,1,1024]{2,1,0:T(1,128)} %broadcast_in_dim.48), calls=%async_computation.16 | async-start | bytes 524288 | tf_op jit(solution)/shard_map/all_to_all | solution.py:20
  450.5 11.5 %all-to-all-done.16 = f32[64,1,1024]{2,1,0:T(1,128)S(1)} async-done(((f32[64,1,1024]{2,1,0:T(1,128)}), f32[64,1,1024]{2,1,0:T(1,128)S(1)}, u32[]{:S(2)}, u32[]{:S(2)}) %all-to-all-start.16) | async-done | bytes 262176 | tf_op jit(solution)/shard_map/all_to_all | solution.py:20
  462.8 92.6 %all-reduce.3.cloned.1.call-done = (bf16[3,512,256]{1,2,0:T(8,128)(2,1)}, bf16[2,512,1152]{1,2,0:T(8,128)(2,1)}, bf16[256,512]{1,0:T(8,128)(2,1)}, bf16[1152,512]{1,0:T(8,128)(2,1)}) async-done(((bf16[3,512,256]{1,2,0:T(8,128)(2,1)}, bf16[2,512,1152]{1,2,0:T(8,128)(2,1)}, bf16[256,512]{1,0:T(8,128)(2,1)}, bf16[1152,512]{1,0:T(8,128)(2,1)}), (bf16[3,512,256]{1,2,0:T(8,128)(2,1)}, ...) | async-done | bytes 4587536 | tf_op jit(solution)/shard_map/psum | solution.py:239
  555.4 1.9 convert_element_type.142
  557.3 2.5 copy.72
  559.9 1.7 convert_element_type.147
  562.4 2.9 copy.73
  (150 shorter events, 28.1 us)
Async XLA Ops:
  7.2 109.1 %copy-start = (bf16[1152,512]{1,0:T(8,128)(2,1)S(1)}, bf16[1152,512]{1,0:T(8,128)(2,1)}, u32[]{:S(2)}) copy-start(bf16[1152,512]{1,0:T(8,128)(2,1)} %param.17) | copy-start | bytes 3538948
  7.2 14.8 %copy-start.29 = (bf16[3,512,256]{2,1,0:T(8,128)(2,1)S(1)}, bf16[3,512,256]{2,1,0:T(8,128)(2,1)}, u32[]{:S(2)}) copy-start(bf16[3,512,256]{2,1,0:T(8,128)(2,1)} %param.12) | copy-start | bytes 2359300
  17.0 17.5 %all-to-all-start.1 = ((bf16[4,256,512]{2,1,0:T(8,128)(2,1)}), bf16[4,256,512]{2,1,0:T(8,128)(2,1)S(1)}, u32[]{:S(2)}, u32[]{:S(2)}) async-start(bf16[4,256,512]{2,1,0:T(8,128)(2,1)} %broadcast_in_dim.41), calls=%async_computation.1 | async-start | bytes 2097152 | tf_op jit(solution)/shard_map/all_to_all | solution.py:20
  34.5 3.7 copy-start.25
  38.1 4.6 copy-start.42
  38.1 19.4 %all-to-all-start.2 = ((bf16[2,512,768]{2,1,0:T(8,128)(2,1)}), bf16[2,512,768]{2,1,0:T(8,128)(2,1)S(1)}, u32[]{:S(2)}, u32[]{:S(2)}) async-start(bf16[2,512,768]{2,1,0:T(8,128)(2,1)} %bitcast.131), calls=%async_computation.2 | async-start | bytes 3145728 | tf_op jit(solution)/shard_map/all_to_all | solution.py:34
  42.0 131.6 %all-gather.5.cloned.1.call-start = ((), (), s32[]{:S(2)}) async-start(), calls=%async_computation.18 | async-start | bytes 7077888 | tf_op jit(solution)/shard_map/all_gather | solution.py:167
  43.3 26.1 %copy-start.35 = (f32[1,256]{1,0:T(1,128)}, f32[1,256]{1,0:T(1,128)S(1)}, u32[]{:S(2)}) copy-start(f32[1,256]{1,0:T(1,128)S(1)} %get-tuple-element.87) | copy-start | bytes 3076
  63.5 5.7 copy-start.11
  64.9 19.4 %copy-start.13 = (f32[512,1,256]{2,0,1:T(8,128)}, f32[512,1,256]{2,0,1:T(8,128)S(1)}, u32[]{:S(2)}) copy-start(f32[512,1,256]{2,0,1:T(8,128)S(1)} %copy.84) | copy-start | bytes 1572868
  64.9 19.4 %copy-start.23 = (bf16[256,512]{1,0:T(8,128)(2,1)S(1)}, bf16[256,512]{1,0:T(8,128)(2,1)}, u32[]{:S(2)}) copy-start(bf16[256,512]{1,0:T(8,128)(2,1)} %param.14) | copy-start | bytes 786436
  65.0 19.8 %copy-start.7 = (f32[512,256]{1,0:T(8,128)}, f32[512,256]{1,0:T(8,128)S(1)}, u32[]{:S(2)}) copy-start(f32[512,256]{1,0:T(8,128)S(1)} %bitcast_multiply_fusion.5) | copy-start | bytes 1572868
  65.6 3.7 collective-permute-start
  69.3 28.7 %copy-start.9 = (f32[512,1,256]{2,0,1:T(8,128)}, f32[512,1,256]{2,0,1:T(8,128)S(1)}, u32[]{:S(2)}) copy-start(f32[512,1,256]{2,0,1:T(8,128)S(1)} %copy.82) | copy-start | bytes 1572868
  71.2 26.9 %copy-start.27 = (bf16[256,512]{1,0:T(8,128)(2,1)S(1)}, bf16[256,512]{1,0:T(8,128)(2,1)}, u32[]{:S(2)}) copy-start(bf16[256,512]{1,0:T(8,128)(2,1)} %param.19) | copy-start | bytes 786436
  84.4 0.8 copy-start.20
  98.0 4.9 copy-start.5
  99.1 3.7 copy-start.16
  99.1 13.4 %all-to-all-start.8 = ((bf16[4,256,512]{2,1,0:T(8,128)(2,1)}), bf16[4,256,512]{2,1,0:T(8,128)(2,1)S(1)}, u32[]{:S(2)}, u32[]{:S(2)}) async-start(bf16[4,256,512]{2,1,0:T(8,128)(2,1)} %broadcast_in_dim.44), calls=%async_computation.8 | async-start | bytes 2097152 | tf_op jit(solution)/shard_map/all_to_all | solution.py:20
  112.5 6.8 %copy-start.26 = (bf16[4,256,512]{2,1,0:T(8,128)(2,1)}, bf16[4,256,512]{2,1,0:T(8,128)(2,1)S(1)}, u32[]{:S(2)}) copy-start(bf16[4,256,512]{2,1,0:T(8,128)(2,1)S(1)} %all-to-all-done.8) | copy-start | bytes 3145732
  113.1 6.2 %all-to-all-start.4 = ((f32[2,1,256]{2,1,0:T(1,128)}), f32[2,1,256]{2,1,0:T(1,128)S(1)}, u32[]{:S(2)}, u32[]{:S(2)}) async-start(f32[2,1,256]{2,1,0:T(1,128)} %broadcast_in_dim.42), calls=%async_computation.4 | async-start | bytes 4096 | tf_op jit(solution)/shard_map/all_to_all | solution.py:20
  119.3 0.6 copy-start.39
  119.8 7.0 %copy-start.32 = (f32[512]{0:T(512)S(1)}, f32[512]{0:T(512)}, u32[]{:S(2)}) copy-start(f32[512]{0:T(512)} %param.15) | copy-start | bytes 6148
  119.9 23.2 %all-to-all-start.9 = ((bf16[2,512,1152]{2,1,0:T(8,128)(2,1)}), bf16[2,512,1152]{2,1,0:T(8,128)(2,1)S(1)}, u32[]{:S(2)}, u32[]{:S(2)}) async-start(bf16[2,512,1152]{2,1,0:T(8,128)(2,1)} %bitcast.129), calls=%async_computation.9 | async-start | bytes 4718592 | tf_op jit(solution)/shard_map/all_to_all | solution.py:34
  126.3 0.6 copy-start.33
  156.9 12.8 %all-to-all-start.6 = ((bf16[2,512,512]{2,1,0:T(8,128)(2,1)}), bf16[2,512,512]{2,1,0:T(8,128)(2,1)}, u32[]{:S(2)}, u32[]{:S(2)}) async-start(bf16[2,512,512]{2,1,0:T(8,128)(2,1)} %bitcast.126), calls=%async_computation.6 | async-start | bytes 2097152 | tf_op jit(solution)/shard_map/all_to_all | solution.py:163
  161.4 99.3 %all-gather.9.cloned.1.call-start = ((), (), s32[]{:S(2)}) async-start(), calls=%async_computation.20 | async-start | bytes 7077888 | tf_op jit(solution)/shard_map/all_gather | solution.py:62
  173.6 5.4 copy-start.3
  179.0 2.2 copy-start.2
  183.9 76.7 %copy-start.18 = (bf16[2,512,1152]{2,1,0:T(8,128)(2,1)S(1)}, bf16[2,512,1152]{2,1,0:T(8,128)(2,1)}, u32[]{:S(2)}) copy-start(bf16[2,512,1152]{2,1,0:T(8,128)(2,1)} %param.16) | copy-start | bytes 7077892
  183.9 118.5 %all-gather.7.cloned.1.call-start = ((), (), s32[]{:S(2)}) async-start(), calls=%async_computation.19 | async-start | bytes 3538944 | tf_op jit(solution)/shard_map/all_gather | solution.py:62
  266.6 40.0 %all-to-all-start.10 = ((bf16[4,256,512]{2,1,0:T(8,128)(2,1)}), bf16[4,256,512]{2,1,0:T(8,128)(2,1)S(1)}, u32[]{:S(2)}, u32[]{:S(2)}) async-start(bf16[4,256,512]{2,1,0:T(8,128)(2,1)} %bitcast.138), calls=%async_computation.10 | async-start | bytes 2097152 | tf_op jit(solution)/shard_map/all_to_all | solution.py:34
  306.6 4.4 copy-start.4
  306.6 4.5 copy-start.34
  306.6 18.5 %all-to-all-start.7 = ((bf16[4,256,512]{2,1,0:T(8,128)(2,1)}), bf16[4,256,512]{2,1,0:T(8,128)(2,1)S(1)}, u32[]{:S(2)}, u32[]{:S(2)}) async-start(bf16[4,256,512]{2,1,0:T(8,128)(2,1)} %bitcast.136), calls=%async_computation.7 | async-start | bytes 2097152 | tf_op jit(solution)/shard_map/all_to_all | solution.py:34
  310.9 20.6 %copy-start.28 = (bf16[256,512]{1,0:T(8,128)(2,1)S(1)}, bf16[256,512]{1,0:T(8,128)(2,1)}, u32[]{:S(2)}) copy-start(bf16[256,512]{1,0:T(8,128)(2,1)} %param.19) | copy-start | bytes 786436
  310.9 20.6 %copy-start.41 = (f32[256]{0:T(256)S(1)}, f32[256]{0:T(256)}, u32[]{:S(2)}) copy-start(f32[256]{0:T(256)} %get-tuple-element.94) | copy-start | bytes 3076
  325.7 5.8 %all-to-all-start.11 = ((f32[2,1,256]{2,1,0:T(1,128)}), f32[2,1,256]{2,1,0:T(1,128)S(1)}, u32[]{:S(2)}, u32[]{:S(2)}) async-start(f32[2,1,256]{2,1,0:T(1,128)} %broadcast_in_dim.45), calls=%async_computation.11 | async-start | bytes 4096 | tf_op jit(solution)/shard_map/all_to_all | solution.py:20
  328.9 68.2 %all-gather.11.cloned.1.call-start = ((), (), s32[]{:S(2)}) async-start(), calls=%async_computation.21 | async-start | bytes 2359296 | tf_op jit(solution)/shard_map/all_gather | solution.py:62
  332.4 14.6 %copy-start.24 = (bf16[256,512]{1,0:T(8,128)(2,1)S(1)}, bf16[256,512]{1,0:T(8,128)(2,1)}, u32[]{:S(2)}) copy-start(bf16[256,512]{1,0:T(8,128)(2,1)} %param.14) | copy-start | bytes 786436
  347.0 8.4 %copy-start.8 = (f32[512,256]{1,0:T(8,128)S(1)}, f32[512,256]{1,0:T(8,128)}, u32[]{:S(2)}) copy-start(f32[512,256]{1,0:T(8,128)} %copy-done.7) | copy-start | bytes 1572868
  347.0 8.4 %copy-start.10 = (f32[512,1,256]{2,0,1:T(8,128)S(1)}, f32[512,1,256]{2,0,1:T(8,128)}, u32[]{:S(2)}) copy-start(f32[512,1,256]{2,0,1:T(8,128)} %copy-done.9) | copy-start | bytes 1572868
  347.1 8.4 %copy-start.19 = (f32[512,256]{1,0:T(8,128)S(1)}, f32[512,256]{1,0:T(8,128)}, u32[]{:S(2)}) copy-start(f32[512,256]{1,0:T(8,128)} %get-tuple-element.75) | copy-start | bytes 1572868
  355.4 5.7 copy-start.14
  355.4 5.7 copy-start.36
  355.4 5.7 copy-start.37
  355.4 5.7 copy-start.38
  356.6 4.7 copy-start.12
  356.6 4.5 collective-permute-start.1
  362.7 4.5 copy-start.15
  362.7 192.7 %all-reduce.3.cloned.1.call-start = ((), (), s32[]{:S(2)}) async-start(), calls=%async_computation.22 | async-start | bytes 9175040 | tf_op jit(solution)/shard_map/psum | solution.py:239
  367.2 6.2 %copy-start.21 = (bf16[1024,256]{1,0:T(8,128)(2,1)S(1)}, bf16[1024,256]{1,0:T(8,128)(2,1)}, u32[]{:S(2)}) copy-start(bf16[1024,256]{1,0:T(8,128)(2,1)} %copy-done.20) | copy-start | bytes 1572868
  400.7 8.0 %copy-start.30 = (bf16[3,512,256]{2,1,0:T(8,128)(2,1)S(1)}, bf16[3,512,256]{2,1,0:T(8,128)(2,1)}, u32[]{:S(2)}) copy-start(bf16[3,512,256]{2,1,0:T(8,128)(2,1)} %param.12) | copy-start | bytes 2359300
  401.4 14.8 %all-to-all-start.17 = ((f32[32,3,256]{2,1,0:T(4,128)}), f32[32,3,256]{2,1,0:T(4,128)S(1)}, u32[]{:S(2)}, u32[]{:S(2)}) async-start(f32[32,3,256]{2,1,0:T(4,128)} %broadcast_in_dim.49), calls=%async_computation.17 | async-start | bytes 262144 | tf_op jit(solution)/shard_map/all_to_all | solution.py:20
  412.1 22.6 %copy-start.6 = (bf16[256,512]{1,0:T(8,128)(2,1)S(1)}, bf16[256,512]{1,0:T(8,128)(2,1)}, u32[]{:S(2)}) copy-start(bf16[256,512]{1,0:T(8,128)(2,1)} %param.10) | copy-start | bytes 786436
  412.1 22.6 %copy-start.31 = (f32[512]{0:T(512)S(1)}, f32[512]{0:T(512)}, u32[]{:S(2)}) copy-start(f32[512]{0:T(512)} %param.11) | copy-start | bytes 6148
  416.2 33.2 %copy-start.40 = (f32[256]{0:T(256)S(1)}, f32[256]{0:T(256)}, u32[]{:S(2)}) copy-start(f32[256]{0:T(256)} %get-tuple-element.92) | copy-start | bytes 3076
  416.2 18.2 %all-to-all-start.14 = ((bf16[4,256,512]{2,1,0:T(8,128)(2,1)}), bf16[4,256,512]{2,1,0:T(8,128)(2,1)S(1)}, u32[]{:S(2)}, u32[]{:S(2)}) async-start(bf16[4,256,512]{2,1,0:T(8,128)(2,1)} %bitcast.137), calls=%async_computation.14 | async-start | bytes 2097152 | tf_op jit(solution)/shard_map/all_to_all | solution.py:34
  435.4 5.8 %all-to-all-start.15 = ((f32[2,1,256]{2,1,0:T(1,128)}), f32[2,1,256]{2,1,0:T(1,128)S(1)}, u32[]{:S(2)}, u32[]{:S(2)}) async-start(f32[2,1,256]{2,1,0:T(1,128)} %broadcast_in_dim.47), calls=%async_computation.15 | async-start | bytes 4096 | tf_op jit(solution)/shard_map/all_to_all | solution.py:20
  442.1 19.9 %all-to-all-start.16 = ((f32[64,1,1024]{2,1,0:T(1,128)}), f32[64,1,1024]{2,1,0:T(1,128)S(1)}, u32[]{:S(2)}, u32[]{:S(2)}) async-start(f32[64,1,1024]{2,1,0:T(1,128)} %broadcast_in_dim.48), calls=%async_computation.16 | async-start | bytes 524288 | tf_op jit(solution)/shard_map/all_to_all | solution.py:20
  555.4 4.5 copy-start.22
  559.9 2.5 copy-start.17
  561.6 3.7 copy-start.1
Sparse Core Ops, SparseCore 0:
  44.4 73.7 all-gather.4
  184.0 76.5 all-gather.8
  262.9 39.5 all-gather.6
  362.8 34.2 all-gather.10
  400.9 154.4 all-reduce.2
where the time goes:
time: 574 us; the launch traced here: 572 us
  waiting for transfers between devices  326 us (57%)
  blocking collectives  67.1 us (12%)
  starting transfers between devices  62.4 us (11%)
  matrix products  41.8 us (7%)
  local copies, waits for them, and re-layouts  31.5 us (5%)
  other arithmetic  28.8 us (5%)
  between operations  14.3 us (2%)
    all_gather x3, waiting for transfers between devices, gather_rows(): return lax.all_gather(value, 'row', axis=0, tiled=True)  127 us
    psum x1, waiting for transfers between devices, per_device(): lax.psum(grad_in_weight.astype(jnp.bfloat16), 'dp').astype(jnp.float32)  92.6 us
    all_to_all x5, waiting for transfers between devices, sent_and_summed(): lax.all_to_all(tiles, axis, split_axis=0, concat_axis=0, tiled=True)  55.7 us
    all_to_all x7, waiting for transfers between devices, from_everyone(): return lax.all_to_all(copies, axis, split_axis=0, concat_axis=0, tiled=True)  40.7 us
    all_to_all x3, blocking collectives, from_everyone(): return lax.all_to_all(copies, axis, split_axis=0, concat_axis=0, tiled=True)  33.2 us
    all_to_all x7, starting transfers between devices, from_everyone(): return lax.all_to_all(copies, axis, split_axis=0, concat_axis=0, tiled=True)  32.9 us
    all_to_all x2, blocking collectives, sent_and_summed(): lax.all_to_all(tiles, axis, split_axis=0, concat_axis=0, tiled=True)  20.7 us
    all_to_all x5, starting transfers between devices, sent_and_summed(): lax.all_to_all(tiles, axis, split_axis=0, concat_axis=0, tiled=True)  20.4 us
  transfers between devices with their start and end apart: 20, of which 16 were waited for; matrix products, arithmetic and copies ran while one was open for 11% of the time, Pallas kernels for 0%

commit v1 on v0

v1 whole, which is shorter than its diff:
```python
import functools

import jax
import jax.numpy as jnp
from jax import lax
from jax.experimental import pallas as pl
from jax.experimental.pallas import tpu as pltpu
from jax.sharding import PartitionSpec as P

MESH = pl.DeviceIdType.MESH
D = 1024
HALF = 512
T = 128
W = 256
H = 1152
EPS = 1e-05
F32 = jnp.float32
BF = jnp.bfloat16

UNITS = (("dn0", 144, 128, 0), ("dn1", 144, 128, 1), ("gt", 32, H, 0), ("up", 32, H, 1), ("oi0", 32, 512, 0), ("oi1", 32, 512, 1))


def mod(a, n):
    return lax.rem(a + 4 * n, n)


def dot(a, b):
    return lax.dot_general(a, b, (((1,), (0,)), ((), ())), preferred_element_type=F32)


def dot_nt(a, b):
    return lax.dot_general(a, b, (((1,), (1,)), ((), ())), preferred_element_type=F32)


def dot_tn(a, b):
    return lax.dot_general(a, b, (((0,), (0,)), ((), ())), preferred_element_type=F32)


def scratch_list():
    s = {}
    dma = pltpu.SemaphoreType.DMA

    def v(name, shape, dtype):
        s[name] = pltpu.VMEM(shape, dtype)

    v("INW", (3, D, W), BF)
    v("OUTW", (W, D), BF)
    v("GUW", (2, D, H), BF)
    v("DNW", (H, D), BF)
    v("X", (T, D), BF)
    v("M", (4, T, 128), BF)
    v("GA", (8, D), F32)
    for n in ("N1", "N2", "COT", "GB"):
        v(n, (4, T, D), BF)
        s[n + "_s"] = dma((4,))
        s[n + "_r"] = dma((4,))
    v("PR", (5, T + 8, W), F32)
    for n in ("GBV", "GCV", "VAL", "CO", "GCONV"):
        v(n, (4, T, W), F32)
    v("GATED", (4, T, W), BF)
    v("FM", (2, 5, T + 8, W), F32)
    v("HID", (T, D), F32)
    v("A", (4, T, H), BF)
    v("GG", (4, T, 2 * H), BF)
    v("GM", (4, T, 3 * W), BF)
    v("SB", (3, T, D), BF)
    v("SBF", (3, T, D), BF)
    v("OWN", (T, D), F32)
    v("OWNF", (T, D), F32)
    for n in ("R1", "R2", "R3", "RF"):
        v(n, (3, T, D), BF)
        s[n + "_s"] = dma((4,))
        s[n + "_r"] = dma((4,))
    v("MIXB", (T, D), BF)
    v("GTB", (T, D), BF)
    v("SM", (8, D), F32)
    v("SMC", (8, D), F32)
    v("SMX", (4, 8, D), F32)
    v("SMY", (4, 8, D), F32)
    v("SMZ", (4, 8, D), F32)
    s["SM_s"] = dma((12,))
    s["SM_r"] = dma((12,))
    s["sw_s"] = dma((10,))
    s["sw_r"] = dma((10,))
    s["ga"] = dma((3,))
    s["w_l"] = dma((4,))
    s["w_s"] = dma((12,))
    s["w_r"] = dma((12,))
    s["halo"] = dma((4,))
    for n, m, k, _ in UNITS:
        v(n + "_W", (2, 4, 4, m, k), BF)
        v(n + "_C", (4, 4, m, k), BF)
        v(n + "_R1", (3, 4, m, k), BF)
        v(n + "_S", (4, m, k), BF)
        v(n + "_R2", (3, m, k), BF)
        v(n + "_O", (2, 4, m, k), BF)
        s[n + "_s"] = dma((14,))
        s[n + "_r"] = dma((14,))
        s[n + "_l"] = dma((2,))
    return s


IN_NAMES = ("tok", "cot", "reach", "gains", "ck", "inw", "outw", "guw", "dnw")
OUT_NAMES = ("o_mixed", "o_gt", "o_small", "o_in", "o_out", "o_gu", "o_dn")


class Refs:
    pass


def kernel(*refs):
    q = Refs()
    names = IN_NAMES + OUT_NAMES + tuple(scratch_list())
    for name, ref in zip(names, refs, strict=True):
        setattr(q, name, ref)

    dp = lax.axis_index("dp")
    r = lax.axis_index("row")
    c = lax.axis_index("col")
    yhi = lax.div(dp, 8)
    x = lax.rem(lax.div(dp, 2), 4)
    k = lax.rem(dp, 2)
    y = yhi * 2 + r
    same = k == r
    other = k != r

    def dev(yhi_=None, x_=None, k_=None, r_=None, c_=None):
        yhi_ = yhi if yhi_ is None else yhi_
        x_ = x if x_ is None else x_
        k_ = k if k_ is None else k_
        return {"dp": yhi_ * 8 + x_ * 2 + k_, "row": r if r_ is None else r_, "col": c if c_ is None else c_}

    def at_y(d):
        to = mod(y + d, 4)
        return dev(yhi_=lax.div(to, 2), r_=lax.rem(to, 2))

    def at_x(d):
        return dev(x_=mod(x + d, 4))

    def at_z(d):
        return dev(c_=mod(c + d, 4))

    mate = dev(k_=1 - k)

    def slot_y(d):
        to = mod(y + d, 4)
        return lax.rem(to, 2) * 2 + lax.div(to, 2)

    def rcopy(src, dst, ss, rs, to):
        return pltpu.make_async_remote_copy(
            src_ref=src, dst_ref=dst, send_sem=ss, recv_sem=rs, device_id=to, device_id_type=MESH
        )

    barrier = pltpu.get_barrier_semaphore()
    friends = [mate, dev(r_=1 - r, k_=1 - k)]
    friends += [f(d) for f in (at_x, at_y, at_z) for d in (1, 2, 3)]
    for to in friends:
        pl.semaphore_signal(barrier, inc=1, device_id=to, device_id_type=MESH)
    pl.semaphore_wait(barrier, len(friends))

    def weight_regions(w):
        if w == 0:
            return (q.inw, q.INW, lambda p, n, a: (q.inw.at[:, pl.ds(p * 128, 128 * n), :], q.INW.at[:, pl.ds(a * HALF + p * 128, 128 * n), :]))
        if w == 1:
            return (q.outw, q.OUTW, lambda p, n, a: (q.outw.at[pl.ds(p * 64, 64 * n), :], q.OUTW.at[pl.ds(p * 64, 64 * n), pl.ds(pl.multiple_of(a * HALF, HALF), HALF)]))
        if w == 2:
            return (q.guw, q.GUW, lambda p, n, a: (q.guw.at[:, pl.ds(p * 128, 128 * n), :], q.GUW.at[:, pl.ds(a * HALF + p * 128, 128 * n), :]))
        return (q.dnw, q.DNW, lambda p, n, a: (q.dnw.at[pl.ds(p * 288, 288 * n), :], q.DNW.at[pl.ds(p * 288, 288 * n), pl.ds(pl.multiple_of(a * HALF, HALF), HALF)]))

    def weight_local(w):
        _, _, region = weight_regions(w)
        src, dst = region(0, 4, r)
        return pltpu.make_async_copy(src, dst, q.w_l.at[w])

    def weight_send(w, s):
        _, _, region = weight_regions(w)
        src, dst = region(k * 2 + s, 1, r)
        return rcopy(src, dst, q.w_s.at[w * 3 + s], q.w_r.at[w * 3 + s], at_y(1 - 2 * s))

    def weight_arrival(w, s):
        _, _, region = weight_regions(w)
        src, _ = region(k * 2 + s, 1, r)
        _, dst = region(k * 2 + s, 1, 1 - r)
        return rcopy(src, dst, q.w_s.at[w * 3 + s], q.w_r.at[w * 3 + s], at_y(1 - 2 * s))

    def weight_pass(w, core):
        _, _, region = weight_regions(w)
        _, dst = region(core * 2, 2, 1 - r)
        return rcopy(dst, dst, q.w_s.at[w * 3 + 2], q.w_r.at[w * 3 + 2], mate)

    def weight_start(w):
        for s in (0, 1):
            weight_send(w, s).start()

    def weight_forward(w):
        for s in (0, 1):
            weight_arrival(w, s).wait_recv()
        weight_pass(w, k).start()

    def weight_ready(w):
        weight_local(w).wait()
        weight_pass(w, 1 - k).wait_recv()

    def weight_end(w):
        for s in (0, 1):
            weight_send(w, s).wait_send()
        weight_pass(w, k).wait_send()

    for w in range(4):
        weight_local(w).start()

    def swap_views(n):
        if n == 0:
            return lambda j: q.tok.at[pl.ds(j * T, T), :], lambda a: q.X.at[:, pl.ds(pl.multiple_of(a * HALF, HALF), HALF)]
        if n == 1:
            return lambda j: q.reach.at[:, j], lambda a: q.M.at[pl.ds(2 * a, 2)]
        return lambda j: q.cot.at[pl.ds(j * T, T), :], lambda a: q.COT.at[c, :, pl.ds(pl.multiple_of(a * HALF, HALF), HALF)]

    def swap_near(n):
        src, dst = swap_views(n)
        return (
            pltpu.make_async_copy(src(k), dst(r), q.sw_r.at[2 * n]),
            rcopy(src(1 - k), dst(r), q.sw_s.at[2 * n], q.sw_r.at[2 * n], mate),
        )

    def swap_far(n, j):
        src, dst = swap_views(n)
        return rcopy(src(j), dst(r), q.sw_s.at[2 * n + j], q.sw_r.at[2 * n + 1], dev(r_=1 - r, k_=j))

    def swap_start(n):
        @pl.when(same)
        def _():
            near, far = swap_near(n)
            near.start()
            far.start()

        @pl.when(other)
        def _():
            swap_far(n, 0).start()
            swap_far(n, 1).start()

    def swap_wait(n):
        src, dst = swap_views(n)

        @pl.when(same)
        def _():
            near, far = swap_near(n)
            near.wait()
            far.wait_send()

        @pl.when(other)
        def _():
            swap_far(n, 0).wait_send()
            swap_far(n, 1).wait_send()
            rcopy(src(1 - k), dst(r), q.sw_s.at[2 * n], q.sw_r.at[2 * n], mate).wait_recv()

        rcopy(src(0), dst(1 - r), q.sw_s.at[2 * n], q.sw_r.at[2 * n + 1], dev(r_=1 - r)).wait_recv()

    def gain_view(a):
        return q.GA.at[:, pl.ds(pl.multiple_of(a * HALF, HALF), HALF)]

    gain_local = pltpu.make_async_copy(q.gains, gain_view(r), q.ga.at[0])
    gain_send = rcopy(q.gains, gain_view(r), q.ga.at[1], q.ga.at[2], dev(r_=1 - r))
    gain_take = rcopy(q.gains, gain_view(1 - r), q.ga.at[1], q.ga.at[2], dev(r_=1 - r))

    swap_start(0)
    gain_local.start()
    gain_send.start()
    weight_start(0)
    swap_start(1)

    def gather(name, d):
        buf = getattr(q, name)
        return rcopy(buf.at[c], buf.at[c], getattr(q, name + "_s").at[d], getattr(q, name + "_r").at[d], at_z(d))

    def gather_start(name):
        for d in (1, 3, 2):
            gather(name, d).start()

    def gather_take(name, d):
        buf = getattr(q, name)
        s = mod(c - d, 4)
        rcopy(buf.at[s], buf.at[s], getattr(q, name + "_s").at[d], getattr(q, name + "_r").at[d], at_z(d)).wait_recv()

    def gather_end(name):
        for d in (1, 3, 2):
            gather(name, d).wait_send()

    def reduce_send(name, send, e):
        buf = getattr(q, name)
        return rcopy(send.at[e - 1], buf.at[e - 1], getattr(q, name + "_s").at[e], getattr(q, name + "_r").at[e], at_z(e))

    def reduce_sum(name, send, own):
        buf = getattr(q, name)
        for e in (1, 3, 2):
            reduce_send(name, send, e).wait()
        return own[...] + (buf[0].astype(F32) + buf[2].astype(F32)) + buf[1].astype(F32)

    def put_part(name, send, own, e, part):
        @pl.when(e == 0)
        def _():
            own[...] = part

        @pl.when(e != 0)
        def _():
            send[e - 1] = part.astype(BF)
            reduce_send(name, send, e).start()

    def arrival(i):
        return i + lax.div(i, 2) - 2 * lax.div(i, 3)

    def far_first(i):
        return mod(2 - i + 3 * lax.div(i, 2) - 2 * lax.div(i, 3), 4)

    def norm_scale(value):
        return lax.rsqrt(jnp.sum(value * value, axis=1, keepdims=True) / D + EPS)

    swap_wait(0)
    gain_local.wait()
    gain_take.wait_recv()
    inputs = q.X[...].astype(F32)
    q.N1[c] = (inputs * norm_scale(inputs) * q.GA[0:1, :]).astype(BF)
    gather_start("N1")
    swap_start(2)
    for w in (1, 2, 3):
        weight_start(w)
    weight_forward(0)
    weight_ready(0)

    @pl.when(k == 0)
    def _():
        q.PR[0, 0:8] = jnp.zeros((8, W), F32)

    def in_step(i, carry):
        d = arrival(i)
        s = mod(c - d, 4)

        @pl.when(i > 0)
        def _():
            gather_take("N1", d)

        rows = q.N1[s]
        b = dot(rows, q.INW[0])
        v = dot(rows, q.INW[2])
        q.GBV[s] = b
        q.VAL[s] = v
        q.PR[s, 8:] = b * v
        q.GCV[s] = dot(rows, q.INW[1])
        return carry

    lax.fori_loop(0, 4, in_step, 0)
    gather_end("N1")

    halo_f = rcopy(q.PR.at[0:4, pl.ds(T, 8)], q.PR.at[pl.ds(k, 4), 0:8], q.halo.at[0], q.halo.at[1], mate)
    halo_ft = rcopy(q.PR.at[0:4, pl.ds(T, 8)], q.PR.at[pl.ds(1 - k, 4), 0:8], q.halo.at[0], q.halo.at[1], mate)
    halo_f.start()
    weight_forward(1)
    swap_wait(2)
    gather_start("COT")
    swap_wait(1)
    halo_f.wait_send()
    halo_ft.wait_recv()
    weight_ready(1)

    def masks(s):
        reach = q.M[s].astype(F32)
        first = jnp.where(reach >= 1.0, 1.0, 0.0)
        second = jnp.where(reach >= 2.0, 1.0, 0.0)
        return jnp.concatenate([first, first], axis=1), jnp.concatenate([second, second], axis=1)

    def conv_step(i, carry):
        e = far_first(i)
        s = mod(c + e, 4)
        m1, m2 = masks(s)
        conv = q.ck[0:1, :] * q.PR[s, pl.ds(8, T)]
        conv = conv + q.ck[1:2, :] * q.PR[s, pl.ds(7, T)] * m1
        conv = conv + q.ck[2:3, :] * q.PR[s, pl.ds(6, T)] * m2
        q.CO[s] = conv
        gated = (q.GCV[s] * conv).astype(BF)
        q.GATED[s] = gated
        put_part("R1", q.SB, q.OWN, e, dot(gated, q.OUTW[...]))
        return carry

    lax.fori_loop(0, 4, conv_step, 0)
    weight_forward(2)
    weight_forward(3)

    hidden = q.X[...].astype(F32) + reduce_sum("R1", q.SB, q.OWN)
    q.HID[...] = hidden
    q.N2[c] = (hidden * norm_scale(hidden) * q.GA[1:2, :]).astype(BF)
    gather_start("N2")
    for d in (1, 3, 2):
        gather_take("COT", d)
    gather_end("COT")
    weight_ready(2)
    weight_ready(3)

    def ffn_step(i, carry):
        d = arrival(i)
        s = mod(c - d, 4)
        e = mod(4 - d, 4)

        @pl.when(i > 0)
        def _():
            gather_take("N2", d)

        rows = q.N2[s]
        gate = dot(rows, q.GUW[0])
        up = dot(rows, q.GUW[1])
        sig = 1.0 / (1.0 + jnp.exp(-gate))
        silu = gate * sig
        q.A[s] = (silu * up).astype(BF)
        ga = dot_nt(q.COT[s], q.DNW[...])
        q.GG[s, :, 0:H] = (ga * up * sig * (1.0 + gate * (1.0 - sig))).astype(BF)
        q.GG[s, :, H:] = (ga * silu).astype(BF)
        part = dot_nt(q.GG[s, :, 0:H], q.GUW[0]) + dot_nt(q.GG[s, :, H:], q.GUW[1])
        put_part("R2", q.SB, q.OWN, e, part)
        return carry

    lax.fori_loop(0, 4, ffn_step, 0)
    gather_end("N2")

    def unit(name):
        return next(u for u in UNITS if u[0] == name)

    def g(name, what):
        return getattr(q, name + "_" + what)

    def core_copy(name, core):
        return rcopy(g(name, "W").at[core], g(name, "C"), g(name, "s").at[0], g(name, "r").at[0], mate)

    def first_copy(name, d):
        w = g(name, "W")
        if unit(name)[3] == 0:
            src, to = w.at[k, :, mod(x + d, 4)], at_x(d)
        else:
            src, to = w.at[k, slot_y(d)], at_y(d)
        return rcopy(src, g(name, "R1").at[d - 1], g(name, "s").at[d], g(name, "r").at[d], to)

    def second_copy(name, d):
        if unit(name)[3] == 0:
            src, to = g(name, "S").at[slot_y(d)], at_y(d)
        else:
            src, to = g(name, "S").at[mod(x + d, 4)], at_x(d)
        return rcopy(src, g(name, "R2").at[d - 1], g(name, "s").at[3 + d], g(name, "r").at[3 + d], to)

    def spread_x(name, d, place):
        o = g(name, "O")
        view = o.at[:, place] if unit(name)[3] == 0 else o.at[yhi, place]
        return rcopy(view, view, g(name, "s").at[6 + d], g(name, "r").at[6 + d], at_x(d))

    def spread_y(name, place):
        o = g(name, "O")
        view = o.at[place, x] if unit(name)[3] == 0 else o.at[place]
        return rcopy(view, view, g(name, "s").at[10], g(name, "r").at[10], at_y(2))

    def core_send(name):
        core_copy(name, 1 - k).start()

    def stage_one(name):
        core_copy(name, 1 - k).wait()
        w, other_part = g(name, "W"), g(name, "C")

        def add(i, carry):
            a, b = lax.div(i, 4), lax.rem(i, 4)
            w[k, a, b] = (w[k, a, b].astype(F32) + other_part[a, b].astype(F32)).astype(BF)
            return carry

        lax.fori_loop(0, 16, add, 0)
        for d in (1, 3, 2):
            first_copy(name, d).start()

    def stage_two(name):
        for d in (1, 3, 2):
            first_copy(name, d).wait()
        w, got, total = g(name, "W"), g(name, "R1"), g(name, "S")

        def add(i, carry):
            mine = w[k, i, x] if unit(name)[3] == 0 else w[k, slot_y(0), i]
            total[i] = (mine.astype(F32) + got[0, i].astype(F32) + got[1, i].astype(F32) + got[2, i].astype(F32)).astype(BF)
            return carry

        lax.fori_loop(0, 4, add, 0)
        for d in (1, 3, 2):
            second_copy(name, d).start()

    def stage_three(name):
        for d in (1, 3, 2):
            second_copy(name, d).wait()
        got, total = g(name, "R2"), g(name, "S")
        mine = total[slot_y(0)] if unit(name)[3] == 0 else total[x]
        g(name, "O")[yhi, x] = (mine.astype(F32) + got[0].astype(F32) + got[1].astype(F32) + got[2].astype(F32)).astype(BF)
        if unit(name)[3] == 0:
            spread_y(name, yhi).start()
        else:
            for d in (1, 3, 2):
                spread_x(name, d, x).start()

    def take_x(name):
        for d in (1, 3, 2):
            spread_x(name, d, x).wait_send()
            spread_x(name, d, mod(x - d, 4)).wait_recv()

    def take_y(name):
        spread_y(name, yhi).wait_send()
        spread_y(name, 1 - yhi).wait_recv()

    def stage_four(name):
        if unit(name)[3] == 0:
            take_y(name)
            for d in (1, 3, 2):
                spread_x(name, d, x).start()
        else:
            take_x(name)
            spread_y(name, yhi).start()

    def results(name, core):
        o = g(name, "O")
        half = unit(name)[3]
        if name in ("dn0", "dn1"):
            at = pl.multiple_of(core * W + half * 128, 128)
            return [(o, q.o_dn.at[:, :, :, pl.ds(at, 128)])]
        if name in ("gt", "up"):
            return [(o, q.o_gu.at[half, core])]
        if name == "oi0":
            at = pl.multiple_of(core * W, W)
            return [(o.at[:, :, :, 0:W], q.o_out.at[:, :, :, pl.ds(at, W)]), (o.at[:, :, :, W:], q.o_in.at[0, core])]
        return [(o.at[:, :, :, 0:W], q.o_in.at[1, core]), (o.at[:, :, :, W:], q.o_in.at[2, core])]

    def stage_five(name):
        if unit(name)[3] == 0:
            take_x(name)
        else:
            take_y(name)
        for n, (src, dst) in enumerate(results(name, k)):
            pltpu.make_async_copy(src, dst, g(name, "l").at[n]).start()
            rcopy(src, dst, g(name, "s").at[11 + n], g(name, "r").at[11 + n], mate).start()

    def stage_six(name):
        for n, (src, dst) in enumerate(results(name, k)):
            pltpu.make_async_copy(src, dst, g(name, "l").at[n]).wait()
            rcopy(src, dst, g(name, "s").at[11 + n], g(name, "r").at[11 + n], mate).wait_send()
        for n, (src, dst) in enumerate(results(name, 1 - k)):
            rcopy(src, dst, g(name, "s").at[11 + n], g(name, "r").at[11 + n], mate).wait_recv()

    def features(ref, a, core):
        at = pl.multiple_of(a * HALF + core * W, W)
        return ref[:, :, pl.ds(at, W)].reshape(4 * T, W)

    def grad_down(core):
        def step(a, carry):
            full = dot_tn(q.A[...].reshape(4 * T, H), features(q.COT, a, core)).astype(BF).reshape(2, 4, 144, W)
            q.dn0_W[core, pl.ds(2 * a, 2)] = full[:, :, :, :128]
            q.dn1_W[core, pl.ds(2 * a, 2)] = full[:, :, :, 128:]
            return carry

        lax.fori_loop(0, 2, step, 0)

    def grad_gate_up(core):
        def step(a, carry):
            rows = features(q.N2, a, core)
            q.gt_W[core, pl.ds(2 * a, 2)] = dot_tn(rows, q.GG[:, :, 0:H].reshape(4 * T, H)).astype(BF).reshape(2, 4, 32, H)
            q.up_W[core, pl.ds(2 * a, 2)] = dot_tn(rows, q.GG[:, :, H:].reshape(4 * T, H)).astype(BF).reshape(2, 4, 32, H)
            return carry

        lax.fori_loop(0, 2, step, 0)

    def grad_out_in(core):
        def step(a, carry):
            rows = features(q.N1, a, core)
            gated = q.GATED[...].reshape(4 * T, W)
            q.oi0_W[core, pl.ds(2 * a, 2), :, :, 0:W] = dot_tn(gated, features(q.GB, a, core)).astype(BF).reshape(2, 4, 32, W)
            into = dot_tn(rows, q.GM[...].reshape(4 * T, 3 * W)).astype(BF).reshape(2, 4, 32, 3 * W)
            q.oi0_W[core, pl.ds(2 * a, 2), :, :, W:] = into[:, :, :, 0:W]
            q.oi1_W[core, pl.ds(2 * a, 2)] = into[:, :, :, W:]
            return carry

        lax.fori_loop(0, 2, step, 0)

    grad_down(1 - k)
    core_send("dn0")
    core_send("dn1")
    grad_gate_up(1 - k)
    core_send("gt")
    core_send("up")
    grad_down(k)

    def norm_back(value, scale, gain, grad):
        weighted = grad * gain
        inner = jnp.sum(weighted * value, axis=1, keepdims=True)
        back = scale * weighted - value * (scale * scale * scale) * inner / D
        return back, jnp.sum(grad * value * scale, axis=0, keepdims=True)

    grad_normed = reduce_sum("R2", q.SB, q.OWN)
    hidden = q.HID[...]
    back, grad_gain = norm_back(hidden, norm_scale(hidden), q.GA[1:2, :], grad_normed)
    q.SM[...] = jnp.zeros((8, D), F32)
    q.SM[1:2, :] = grad_gain
    grad_hidden = q.COT[c].astype(F32) + back
    q.GB[c] = grad_hidden.astype(BF)
    q.OWN[...] = grad_hidden
    gather_start("GB")
    grad_gate_up(k)
    stage_one("dn0")
    stage_one("dn1")
    stage_one("gt")
    stage_one("up")

    @pl.when(k == 1)
    def _():
        q.FM[0, 4, pl.ds(T, 8)] = jnp.zeros((8, W), F32)
        q.FM[1, 4, pl.ds(T, 8)] = jnp.zeros((8, W), F32)

    def conv_back_step(i, carry):
        d = arrival(i)
        s = mod(c - d, 4)

        @pl.when(i > 0)
        def _():
            gather_take("GB", d)

        grad_gated = dot_nt(q.GB[s], q.OUTW[...])
        q.GM[s, :, W : 2 * W] = (grad_gated * q.CO[s]).astype(BF)
        grad_conv = grad_gated * q.GCV[s]
        q.GCONV[s] = grad_conv
        m1, m2 = masks(s)
        q.FM[0, s + 1, 0:T] = grad_conv * m1
        q.FM[1, s + 1, 0:T] = grad_conv * m2
        return carry

    lax.fori_loop(0, 4, conv_back_step, 0)
    gather_end("GB")
    halo_b = rcopy(q.FM.at[:, 1:5, 0:8], q.FM.at[:, pl.ds(k, 4), pl.ds(T, 8)], q.halo.at[2], q.halo.at[3], mate)
    halo_bt = rcopy(q.FM.at[:, 1:5, 0:8], q.FM.at[:, pl.ds(1 - k, 4), pl.ds(T, 8)], q.halo.at[2], q.halo.at[3], mate)
    halo_b.start()
    halo_b.wait_send()
    halo_bt.wait_recv()

    def product_back_step(i, carry):
        e = far_first(i)
        s = mod(c + e, 4)
        grad_conv = q.GCONV[s]
        grad_product = q.ck[0:1, :] * grad_conv
        grad_product = grad_product + q.ck[1:2, :] * q.FM[0, s + 1, pl.ds(1, T)]
        grad_product = grad_product + q.ck[2:3, :] * q.FM[1, s + 1, pl.ds(2, T)]
        q.SM[2:3, 0:W] += jnp.sum(grad_conv * q.PR[s, pl.ds(8, T)], axis=0, keepdims=True)
        q.SM[3:4, 0:W] += jnp.sum(q.FM[0, s + 1, pl.ds(0, T)] * q.PR[s, pl.ds(7, T)], axis=0, keepdims=True)
        q.SM[4:5, 0:W] += jnp.sum(q.FM[1, s + 1, pl.ds(0, T)] * q.PR[s, pl.ds(6, T)], axis=0, keepdims=True)
        q.GM[s, :, 0:W] = (grad_product * q.VAL[s]).astype(BF)
        q.GM[s, :, 2 * W :] = (grad_product * q.GBV[s]).astype(BF)
        part = dot_nt(q.GM[s, :, 0:W], q.INW[0]) + dot_nt(q.GM[s, :, W : 2 * W], q.INW[1]) + dot_nt(q.GM[s, :, 2 * W :], q.INW[2])
        put_part("R3", q.SB, q.OWNF, e, part)
        return carry

    lax.fori_loop(0, 4, product_back_step, 0)
    grad_out_in(1 - k)
    core_send("oi0")
    core_send("oi1")
    grad_out_in(k)

    grad_normed = reduce_sum("R3", q.SB, q.OWNF)

    def ffn_out_step(i, carry):
        e = far_first(i)
        s = mod(c + e, 4)
        put_part("RF", q.SBF, q.OWNF, e, dot(q.A[s], q.DNW[...]))
        return carry

    lax.fori_loop(0, 4, ffn_out_step, 0)
    stage_one("oi0")
    stage_one("oi1")

    def home(n):
        buf, out = ((q.MIXB, q.o_mixed), (q.GTB, q.o_gt))[n]
        base = 6 + 2 * n
        halves = lambda a: buf.at[:, pl.ds(pl.multiple_of(a * HALF, HALF), HALF)]
        rows = lambda j: out.at[pl.ds(j * T, T), :]
        near_local = pltpu.make_async_copy(halves(r), rows(k), q.sw_r.at[base])
        near_far = rcopy(halves(r), rows(k), q.sw_s.at[base], q.sw_r.at[base + 1], mate)
        away = rcopy(halves(1 - r), rows(k), q.sw_s.at[base + 1], q.sw_r.at[base + k], dev(r_=1 - r, k_=r))
        return halves, rows, base, near_local, near_far, away

    def home_start(n):
        halves, rows, base, near_local, near_far, away = home(n)

        @pl.when(same)
        def _():
            near_local.start()

        @pl.when(other)
        def _():
            near_far.start()

        away.start()

    def home_wait(n):
        halves, rows, base, near_local, near_far, away = home(n)

        @pl.when(same)
        def _():
            near_local.wait()
            rcopy(halves(r), rows(1 - k), q.sw_s.at[base], q.sw_r.at[base + 1], mate).wait_recv()

        @pl.when(other)
        def _():
            near_far.wait_send()
            for j in (0, 1):
                rcopy(halves(r), rows(j), q.sw_s.at[base], q.sw_r.at[base + j], dev(r_=1 - r)).wait_recv()

        away.wait_send()

    inputs = q.X[...].astype(F32)
    back, grad_gain = norm_back(inputs, norm_scale(inputs), q.GA[0:1, :], grad_normed)
    q.SM[0:1, :] = grad_gain
    q.GTB[...] = (q.OWN[...] + back).astype(BF)
    home_start(1)

    small_core = rcopy(q.SM, q.SMC, q.SM_s.at[0], q.SM_r.at[0], mate)
    small_core.start()
    for name in ("dn0", "dn1", "gt", "up"):
        stage_two(name)
    small_core.wait()

    def small_step(buf, me, base, target, value, rows):
        buf[me] = value
        for d in (1, 2, 3):
            rcopy(buf.at[me], buf.at[me], q.SM_s.at[base + d - 1], q.SM_r.at[base + d - 1], target(d)).start()

    def small_take(buf, me, base, target):
        for d in (1, 2, 3):
            rcopy(buf.at[me], buf.at[me], q.SM_s.at[base + d - 1], q.SM_r.at[base + d - 1], target(d)).wait_send()
            src = mod(me - d, 4)
            rcopy(buf.at[src], buf.at[src], q.SM_s.at[base + d - 1], q.SM_r.at[base + d - 1], target(d)).wait_recv()
        return (buf[0] + buf[1]) + (buf[2] + buf[3])

    small_step(q.SMX, x, 1, at_x, q.SM[...] + q.SMC[...], 8)
    for name in ("dn0", "dn1", "gt", "up"):
        stage_three(name)
    stage_two("oi0")
    stage_two("oi1")
    total = small_take(q.SMX, x, 1, at_x)
    small_step(q.SMY, y, 4, at_y, total, 8)
    q.MIXB[...] = (q.HID[...] + reduce_sum("RF", q.SBF, q.OWNF)).astype(BF)
    home_start(0)
    for name in ("dn0", "dn1", "gt", "up"):
        stage_four(name)
    stage_three("oi0")
    stage_three("oi1")
    total = small_take(q.SMY, y, 4, at_y)
    small_step(q.SMZ, c, 7, at_z, total, 8)
    stage_four("oi0")
    stage_four("oi1")
    for name in ("dn0", "dn1", "gt", "up"):
        stage_five(name)
    q.o_small[...] = total
    total = small_take(q.SMZ, c, 7, at_z)
    q.o_small[0:2, :] = total[0:2, :]
    stage_five("oi0")
    stage_five("oi1")
    home_wait(0)
    home_wait(1)
    gain_send.wait_send()
    for w in range(4):
        weight_end(w)
    for name in ("dn0", "dn1", "gt", "up", "oi0", "oi1"):
        stage_six(name)


def per_device(
    tokens,
    mixer_gain,
    in_weight,
    conv_kernel,
    out_weight,
    ffn_gain,
    gate_up_weight,
    down_weight,
    conv_reach,
    cotangent,
):
    reach = jnp.broadcast_to(conv_reach.astype(BF).reshape(2, 2, T, 1), (2, 2, T, 128))
    gains = jnp.concatenate([mixer_gain[None], ffn_gain[None], jnp.zeros((6, HALF), F32)], axis=0)
    hbm = pl.BlockSpec(memory_space=pl.ANY)
    vmem = pl.BlockSpec(memory_space=pltpu.VMEM)
    mixed, grad_tokens, small, g_in, g_out, g_gu, g_dn = pl.pallas_call(
        kernel,
        out_shape=(
            jax.ShapeDtypeStruct((2 * T, HALF), BF),
            jax.ShapeDtypeStruct((2 * T, HALF), BF),
            jax.ShapeDtypeStruct((8, D), F32),
            jax.ShapeDtypeStruct((3, 2, 2, 4, 32, W), BF),
            jax.ShapeDtypeStruct((2, 4, 32, HALF), BF),
            jax.ShapeDtypeStruct((2, 2, 2, 4, 32, H), BF),
            jax.ShapeDtypeStruct((2, 4, 144, HALF), BF),
        ),
        in_specs=[hbm, hbm, hbm, hbm, vmem, hbm, hbm, hbm, hbm],
        out_specs=(hbm, hbm, vmem, hbm, hbm, hbm, hbm),
        scratch_shapes=list(scratch_list().values()),
        compiler_params=pltpu.CompilerParams(
            collective_id=0, has_side_effects=True, vmem_limit_bytes=60 * 2**20
        ),
        name="block_step",
    )(tokens, cotangent, reach, gains, conv_kernel, in_weight, out_weight, gate_up_weight, down_weight)
    mine = lax.dynamic_slice_in_dim(small, lax.axis_index("row") * HALF, HALF, axis=1)
    return (
        mixed,
        grad_tokens.astype(F32),
        mine[0],
        g_in.reshape(3, HALF, W).astype(F32),
        small[2:5, :W],
        g_out.reshape(W, HALF).astype(F32),
        mine[1],
        g_gu.reshape(2, HALF, H).astype(F32),
        g_dn.reshape(H, HALF).astype(F32),
    )


def solution(mesh):
    return jax.shard_map(
        per_device,
        mesh=mesh,
        in_specs=(
            P(("dp", "col"), "row"),
            P("row"),
            P(None, "row", "col"),
            P(None, "col"),
            P("col", "row"),
            P("row"),
            P(None, "row", "col"),
            P("col", "row"),
            P(("dp", "row")),
            P(("dp", "col"), "row"),
        ),
        out_specs=(
            P(("dp", "col"), "row"),
            P(("dp", "col"), "row"),
            P("row"),
            P(None, "row", "col"),
            P(None, "col"),
            P("col", "row"),
            P("row"),
            P(None, "row", "col"),
            P("col", "row"),
        ),
        check_vma=False,
    )
```

time: 574 us -> 179 us (0.31)
  waiting for transfers between devices: 326 us -> 0 us
  Pallas kernels: 0 us -> 162 us
  blocking collectives: 67.1 us -> 0 us
  starting transfers between devices: 62.4 us -> 0 us
  matrix products: 41.8 us -> 0 us
  local copies, waits for them, and re-layouts: 31.5 us -> 4.34 us
  other arithmetic: 28.8 us -> 11.2 us
  between operations: 14.3 us -> 0.67 us
    pallas_call x0 -> x1, Pallas kernels: none -> 162 us  [per_device(): pl.pallas_call(kernel, out_shape=(jax.ShapeDtypeStruct((2 * T, HALF), BF)...]
    all_gather x4 -> x0, waiting for transfers between devices: 127 us -> none  [the longest x3 127 us: gather_rows(): return lax.all_gather(value, 'row', axis=0, tiled=True)]
    all_to_all x13 -> x0, waiting for transfers between devices: 103 us -> none  [the longest x5 55.7 us: sent_and_summed(): lax.all_to_all(tiles, axis, split_axis=0, concat_axis=0, tiled=True)]
    psum x1 -> x0, waiting for transfers between devices: 92.6 us -> none  [per_device(): lax.psum(grad_in_weight.astype(jnp.bfloat16), 'dp').astype(jnp.float32)]
    all_to_all x13 -> x0, starting transfers between devices: 57.7 us -> none  [the longest x7 32.9 us: from_everyone(): return lax.all_to_all(copies, axis, split_axis=0, concat_axis=0, tiled=True)]
    all_to_all x5 -> x0, blocking collectives: 53.9 us -> none  [the longest x3 33.2 us: from_everyone(): return lax.all_to_all(copies, axis, split_axis=0, concat_axis=0, tiled=True)]
    dot_general x12 -> x0, matrix products: 41.8 us -> none  [the longest x2 9.37 us: project_back(): jnp.einsum('tkf,kdf->td', parts, weight, preferred_element_type=jnp.float32)]
    all_gather x1 -> x0, blocking collectives: 13.2 us -> none  [gather_rows(): return lax.all_gather(value, 'row', axis=0, tiled=True)]
  transfers between devices with their start and end apart: 20 -> 0, of which waited for: 16 -> 0; matrix products, arithmetic and copies ran while one was open for 11% -> 0% of each run, Pallas kernels for 0% -> 0%
where the time goes in v1:
time: 179 us; the launch traced here: 178 us
  Pallas kernels  162 us (91%)
  other arithmetic  11.2 us (6%)
  local copies, waits for them, and re-layouts  4.34 us (2%)
    pallas_call x1, Pallas kernels, per_device(): pl.pallas_call(kernel, out_shape=(jax.ShapeDtypeStruct((2 * T, HALF), BF)...  162 us
    convert_element_type x1, other arithmetic, per_device(): g_gu.reshape(2, HALF, H).astype(F32)  4.25 us

profile of v1, /device:TPU:1, one launch (start us, length us, event | category | flops | bytes accessed | tf_op | source)
XLA Modules:
  0.0 177.9 jit_solution(5592256945061318040)
XLA Ops:
  0.6 0.7 convert_element_type.30
  1.3 0.8 broadcast_in_dim.17.refs_2_
  2.1 0.1 pad.2.clone
  2.2 1.4 maximum_maximum_fusion.refs_3_
  3.6 161.7 %block_step.1 = (bf16[256,512]{1,0:T(8,128)(2,1)}, bf16[256,512]{1,0:T(8,128)(2,1)}, f32[8,1024]{1,0:T(8,128)}, bf16[3,2,2,4,32,256]{5,4,3,2,1,0:T(8,128)(2,1)},...) custom-call(bf16[256,512]{1,0:T(8,128)(2,1)} %refs_0_.1, ...), custom_call_target="tpu_custom_call" | custom-call | tf_op jit(solution)/shard_map/block_step/pallas_call | solution.py:785
  165.3 1.5 fusion
  166.8 1.3 slice.10
  168.1 0.0 copy-start
  168.1 4.3 %bitcast_convert_fusion = f32[2,512,1152]{2,1,0:T(8,128)} fusion(bf16[2,2,2,4,32,1152]{5,4,3,2,1,0:T(8,128)(2,1)} %get-tuple-element.21), kind=kLoop, calls=%fused_computation | loop fusion | flops 1179648 | bytes 7077888 | tf_op jit(solution)/shard_map/convert_element_type | solution.py:813
  172.3 0.0 copy-start.1
  172.3 0.0 copy-done
  172.3 0.0 copy-start.3
  172.3 1.8 %bitcast_convert_fusion.1 = f32[1152,512]{1,0:T(8,128)} fusion(bf16[2,4,144,512]{3,2,1,0:T(8,128)(2,1)S(1)} %copy-done), kind=kLoop, calls=%fused_computation.1 | loop fusion | flops 589824 | bytes 3538944 | tf_op jit(solution)/shard_map/convert_element_type | solution.py:814
  174.1 0.0 copy-start.2
  174.1 0.0 copy-start.4
  174.1 0.0 copy-done.1
  174.1 1.3 bitcast_convert_fusion.2
  175.5 0.0 copy-done.3
  175.5 0.9 bitcast_convert_fusion.3
  176.3 0.0 copy-done.2
  176.4 0.9 convert_element_type.31
  177.2 0.0 copy-done.4
  177.2 0.7 copy.20
  (1 shorter events, 0.0 us)
Async XLA Ops:
  168.1 4.3 %copy-start = (bf16[2,4,144,512]{3,2,1,0:T(8,128)(2,1)S(1)}, bf16[2,4,144,512]{3,2,1,0:T(8,128)(2,1)}, u32[]{:S(2)}) copy-start(bf16[2,4,144,512]{3,2,1,0:T(8,128)(2,1)} %get-tuple-element.22) | copy-start | bytes 3538948
  172.3 1.8 %copy-start.1 = (bf16[3,2,2,4,32,256]{5,4,3,2,1,0:T(8,128)(2,1)S(1)}, bf16[3,2,2,4,32,256]{5,4,3,2,1,0:T(8,128)(2,1)}, u32[]{:S(2)}) copy-start(bf16[3,2,2,4,32,256]{5,4,3,2,1,0:T(8,128)(2,1)} %get-tuple-element.19) | copy-start | bytes 2359300
  172.3 3.1 %copy-start.3 = (bf16[2,4,32,512]{3,2,1,0:T(8,128)(2,1)S(1)}, bf16[2,4,32,512]{3,2,1,0:T(8,128)(2,1)}, u32[]{:S(2)}) copy-start(bf16[2,4,32,512]{3,2,1,0:T(8,128)(2,1)} %get-tuple-element.20) | copy-start | bytes 786436
  174.1 2.2 %copy-start.2 = (bf16[256,512]{1,0:T(8,128)(2,1)S(1)}, bf16[256,512]{1,0:T(8,128)(2,1)}, u32[]{:S(2)}) copy-start(bf16[256,512]{1,0:T(8,128)(2,1)} %get-tuple-element.17) | copy-start | bytes 786436
  174.1 3.1 %copy-start.4 = (bf16[256,512]{1,0:T(8,128)(2,1)S(1)}, bf16[256,512]{1,0:T(8,128)(2,1)}, u32[]{:S(2)}) copy-start(bf16[256,512]{1,0:T(8,128)(2,1)} %get-tuple-element.34) | copy-start | bytes 786436

commit v2 on v1

--- a/solution.py
+++ b/solution.py
@@ -44,33 +44,40 @@
         s[name] = pltpu.VMEM(shape, dtype)
 
     v("INW", (3, D, W), BF)
-    v("OUTW", (W, D), BF)
+    v("OUTF", (4, 4, 2, 32, D), BF)
+    s["o_s"] = dma((8,))
+    s["o_r"] = dma((8,))
+    s["o_l"] = dma((1,))
     v("GUW", (2, D, H), BF)
     v("DNW", (H, D), BF)
-    v("X", (T, D), BF)
     v("M", (4, T, 128), BF)
     v("GA", (8, D), F32)
-    for n in ("N1", "N2", "COT", "GB"):
-        v(n, (4, T, D), BF)
-        s[n + "_s"] = dma((4,))
-        s[n + "_r"] = dma((4,))
+    for n in ("XF", "COT", "GB", "GF"):
+        v(n, (4, T, D) if n != "GF" else (4, 4 * T, W), BF)
+        s[n + "_s"] = dma((6,))
+        s[n + "_r"] = dma((6,))
+    v("N1", (4, T, D), BF)
+    v("N2", (4, T, D), BF)
+    v("GGS", (4, T, W), BF)
+    v("GGR", (4, T, W), BF)
+    s["GG_s"] = dma((4,))
+    s["GG_r"] = dma((4,))
     v("PR", (5, T + 8, W), F32)
     for n in ("GBV", "GCV", "VAL", "CO", "GCONV"):
         v(n, (4, T, W), F32)
-    v("GATED", (4, T, W), BF)
     v("FM", (2, 5, T + 8, W), F32)
     v("HID", (T, D), F32)
     v("A", (4, T, H), BF)
     v("GG", (4, T, 2 * H), BF)
     v("GM", (4, T, 3 * W), BF)
-    v("SB", (3, T, D), BF)
-    v("SBF", (3, T, D), BF)
     v("OWN", (T, D), F32)
     v("OWNF", (T, D), F32)
-    for n in ("R1", "R2", "R3", "RF"):
-        v(n, (3, T, D), BF)
-        s[n + "_s"] = dma((4,))
-        s[n + "_r"] = dma((4,))
+    for n in ("R2", "R3", "RF"):
+        v(n, (2, T, D), BF)
+        v(n + "_T", (2, T // 2, D), BF)
+        v(n + "_B", (3, T, D), BF)
+        s[n + "_s"] = dma((6,))
+        s[n + "_r"] = dma((6,))
     v("MIXB", (T, D), BF)
     v("GTB", (T, D), BF)
     v("SM", (8, D), F32)
@@ -161,8 +168,6 @@
     def weight_regions(w):
         if w == 0:
             return (q.inw, q.INW, lambda p, n, a: (q.inw.at[:, pl.ds(p * 128, 128 * n), :], q.INW.at[:, pl.ds(a * HALF + p * 128, 128 * n), :]))
-        if w == 1:
-            return (q.outw, q.OUTW, lambda p, n, a: (q.outw.at[pl.ds(p * 64, 64 * n), :], q.OUTW.at[pl.ds(p * 64, 64 * n), pl.ds(pl.multiple_of(a * HALF, HALF), HALF)]))
         if w == 2:
             return (q.guw, q.GUW, lambda p, n, a: (q.guw.at[:, pl.ds(p * 128, 128 * n), :], q.GUW.at[:, pl.ds(a * HALF + p * 128, 128 * n), :]))
         return (q.dnw, q.DNW, lambda p, n, a: (q.dnw.at[pl.ds(p * 288, 288 * n), :], q.DNW.at[pl.ds(p * 288, 288 * n), pl.ds(pl.multiple_of(a * HALF, HALF), HALF)]))
@@ -206,12 +211,56 @@
             weight_send(w, s).wait_send()
         weight_pass(w, k).wait_send()
 
-    for w in range(4):
+    for w in (0, 2, 3):
         weight_local(w).start()
+
+    half = lambda a: pl.ds(pl.multiple_of(a * HALF, HALF), HALF)
+    out_own = q.outw.at[pl.ds(x * 64 + k * 32, 32), :]
+    out_local = pltpu.make_async_copy(out_own, q.OUTF.at[c, x, k, :, half(r)], q.o_l.at[0])
+
+    def out_row(a):
+        return rcopy(out_own, q.OUTF.at[c, x, k, :, half(a)], q.o_s.at[0], q.o_r.at[0], dev(r_=1 - r))
+
+    def out_col(d, a):
+        view = q.OUTF.at[a, x, k]
+        return rcopy(view, view, q.o_s.at[d], q.o_r.at[d], at_z(d))
+
+    def out_x(d, a):
+        view = q.OUTF.at[:, a, k]
+        return rcopy(view, view, q.o_s.at[3 + d], q.o_r.at[3 + d], at_x(d))
+
+    def out_core(core):
+        view = q.OUTF.at[:, :, core]
+        return rcopy(view, view, q.o_s.at[7], q.o_r.at[7], mate)
+
+    def out_stage_col():
+        out_local.wait()
+        out_row(1 - r).wait_recv()
+        for d in (1, 3, 2):
+            out_col(d, c).start()
+
+    def out_stage_x():
+        for d in (1, 3, 2):
+            out_col(d, mod(c - d, 4)).wait_recv()
+        for d in (1, 3, 2):
+            out_x(d, x).start()
+
+    def out_stage_core():
+        for d in (1, 3, 2):
+            out_x(d, mod(x - d, 4)).wait_recv()
+        out_core(k).start()
+
+    def out_ready():
+        out_core(1 - k).wait_recv()
+        out_row(r).wait_send()
+        for d in (1, 2, 3):
+            out_col(d, c).wait_send()
+            out_x(d, x).wait_send()
+        out_core(k).wait_send()
 
     def swap_views(n):
         if n == 0:
-            return lambda j: q.tok.at[pl.ds(j * T, T), :], lambda a: q.X.at[:, pl.ds(pl.multiple_of(a * HALF, HALF), HALF)]
+            return lambda j: q.tok.at[pl.ds(j * T, T), :], lambda a: q.XF.at[c, :, pl.ds(pl.multiple_of(a * HALF, HALF), HALF)]
         if n == 1:
             return lambda j: q.reach.at[:, j], lambda a: q.M.at[pl.ds(2 * a, 2)]
         return lambda j: q.cot.at[pl.ds(j * T, T), :], lambda a: q.COT.at[c, :, pl.ds(pl.multiple_of(a * HALF, HALF), HALF)]
@@ -266,45 +315,102 @@
     swap_start(0)
     gain_local.start()
     gain_send.start()
+    out_local.start()
+    out_row(r).start()
     weight_start(0)
     swap_start(1)
 
-    def gather(name, d):
+    def gather(name, n, a):
         buf = getattr(q, name)
-        return rcopy(buf.at[c], buf.at[c], getattr(q, name + "_s").at[d], getattr(q, name + "_r").at[d], at_z(d))
-
-    def gather_start(name):
-        for d in (1, 3, 2):
-            gather(name, d).start()
+        rows = buf.shape[1] // 2
+        h = (0, 1, 1, 0, 0, 1)[n]
+        view = buf.at[a, pl.ds(h * rows, rows)]
+        return rcopy(view, view, getattr(q, name + "_s").at[n], getattr(q, name + "_r").at[n], at_z(3 if n in (1, 3, 5) else 1))
+
+    def gather_start(name, parts=(0, 1, 2, 3)):
+        for n in parts:
+            gather(name, n, c).start()
+
+    def gather_pass(name):
+        gather(name, 0, mod(c - 1, 4)).wait_recv()
+        gather(name, 4, mod(c - 1, 4)).start()
+        gather(name, 1, mod(c + 1, 4)).wait_recv()
+        gather(name, 5, mod(c + 1, 4)).start()
 
     def gather_take(name, d):
+        if d == 1:
+            gather(name, 2, mod(c - 1, 4)).wait_recv()
+        elif d == 3:
+            gather(name, 3, mod(c + 1, 4)).wait_recv()
+        else:
+            gather(name, 4, mod(c + 2, 4)).wait_recv()
+            gather(name, 5, mod(c + 2, 4)).wait_recv()
+
+    def gather_step(name, i):
+        for n, d in ((1, 1), (2, 3), (3, 2)):
+
+            @pl.when(i == n)
+            def _():
+                if n == 1:
+                    gather_pass(name)
+                gather_take(name, d)
+
+    def gather_end(name):
+        for n in (0, 1, 2, 3):
+            gather(name, n, c).wait_send()
+        gather(name, 4, mod(c - 1, 4)).wait_send()
+        gather(name, 5, mod(c + 1, 4)).wait_send()
+
+    HT = T // 2
+
+    def reduce_copy(name, n):
+        buf, mid, send = getattr(q, name), getattr(q, name + "_T"), getattr(q, name + "_B")
+        src, dst, d = (
+            (send.at[1, 0:HT], mid.at[0], 1),
+            (send.at[1, HT:T], mid.at[1], 3),
+            (send.at[0, HT:T], buf.at[0, HT:T], 1),
+            (send.at[0, 0:HT], buf.at[0, 0:HT], 1),
+            (send.at[2, 0:HT], buf.at[1, 0:HT], 3),
+            (send.at[2, HT:T], buf.at[1, HT:T], 3),
+        )[n]
+        return rcopy(src, dst, getattr(q, name + "_s").at[n], getattr(q, name + "_r").at[n], at_z(d))
+
+    def reduce_sum(name, own):
         buf = getattr(q, name)
-        s = mod(c - d, 4)
-        rcopy(buf.at[s], buf.at[s], getattr(q, name + "_s").at[d], getattr(q, name + "_r").at[d], at_z(d)).wait_recv()
-
-    def gather_end(name):
-        for d in (1, 3, 2):
-            gather(name, d).wait_send()
-
-    def reduce_send(name, send, e):
-        buf = getattr(q, name)
-        return rcopy(send.at[e - 1], buf.at[e - 1], getattr(q, name + "_s").at[e], getattr(q, name + "_r").at[e], at_z(e))
-
-    def reduce_sum(name, send, own):
-        buf = getattr(q, name)
-        for e in (1, 3, 2):
-            reduce_send(name, send, e).wait()
-        return own[...] + (buf[0].astype(F32) + buf[2].astype(F32)) + buf[1].astype(F32)
-
-    def put_part(name, send, own, e, part):
+        for n in (2, 4, 3, 5):
+            reduce_copy(name, n).wait_recv()
+        for n in range(6):
+            reduce_copy(name, n).wait_send()
+        return own[...] + (buf[0].astype(F32) + buf[1].astype(F32))
+
+    def put_part(name, own, e, part):
+        mid, send = getattr(q, name + "_T"), getattr(q, name + "_B")
+
         @pl.when(e == 0)
         def _():
             own[...] = part
 
-        @pl.when(e != 0)
-        def _():
-            send[e - 1] = part.astype(BF)
-            reduce_send(name, send, e).start()
+        @pl.when(e == 2)
+        def _():
+            send[1] = part.astype(BF)
+            reduce_copy(name, 0).start()
+            reduce_copy(name, 1).start()
+
+        @pl.when(e == 1)
+        def _():
+            send[0, HT:T] = part[HT:].astype(BF)
+            reduce_copy(name, 2).start()
+            reduce_copy(name, 0).wait_recv()
+            send[0, 0:HT] = (part[:HT] + mid[0].astype(F32)).astype(BF)
+            reduce_copy(name, 3).start()
+
+        @pl.when(e == 3)
+        def _():
+            send[2, 0:HT] = part[:HT].astype(BF)
+            reduce_copy(name, 4).start()
+            reduce_copy(name, 1).wait_recv()
+            send[2, HT:T] = (part[HT:] + mid[1].astype(F32)).astype(BF)
+            reduce_copy(name, 5).start()
 
     def arrival(i):
         return i + lax.div(i, 2) - 2 * lax.div(i, 3)
@@ -316,14 +422,13 @@
         return lax.rsqrt(jnp.sum(value * value, axis=1, keepdims=True) / D + EPS)
 
     swap_wait(0)
+    gather_start("XF")
+    swap_start(2)
+    for w in (2, 3):
+        weight_start(w)
+    out_stage_col()
     gain_local.wait()
     gain_take.wait_recv()
-    inputs = q.X[...].astype(F32)
-    q.N1[c] = (inputs * norm_scale(inputs) * q.GA[0:1, :]).astype(BF)
-    gather_start("N1")
-    swap_start(2)
-    for w in (1, 2, 3):
-        weight_start(w)
     weight_forward(0)
     weight_ready(0)
 
@@ -332,13 +437,10 @@
         q.PR[0, 0:8] = jnp.zeros((8, W), F32)
 
     def in_step(i, carry):
-        d = arrival(i)
-        s = mod(c - d, 4)
-
-        @pl.when(i > 0)
-        def _():
-            gather_take("N1", d)
-
+        s = mod(c - arrival(i), 4)
+        gather_step("XF", i)
+        inputs = q.XF[s].astype(F32)
+        q.N1[s] = (inputs * norm_scale(inputs) * q.GA[0:1, :]).astype(BF)
         rows = q.N1[s]
         b = dot(rows, q.INW[0])
         v = dot(rows, q.INW[2])
@@ -349,18 +451,15 @@
         return carry
 
     lax.fori_loop(0, 4, in_step, 0)
-    gather_end("N1")
-
     halo_f = rcopy(q.PR.at[0:4, pl.ds(T, 8)], q.PR.at[pl.ds(k, 4), 0:8], q.halo.at[0], q.halo.at[1], mate)
     halo_ft = rcopy(q.PR.at[0:4, pl.ds(T, 8)], q.PR.at[pl.ds(1 - k, 4), 0:8], q.halo.at[0], q.halo.at[1], mate)
     halo_f.start()
-    weight_forward(1)
+    gather_end("XF")
+    out_stage_x()
     swap_wait(2)
-    gather_start("COT")
     swap_wait(1)
     halo_f.wait_send()
     halo_ft.wait_recv()
-    weight_ready(1)
 
     def masks(s):
         reach = q.M[s].astype(F32)
@@ -368,42 +467,45 @@
         second = jnp.where(reach >= 2.0, 1.0, 0.0)
         return jnp.concatenate([first, first], axis=1), jnp.concatenate([second, second], axis=1)
 
-    def conv_step(i, carry):
-        e = far_first(i)
-        s = mod(c + e, 4)
+    def conv_step(s, carry):
         m1, m2 = masks(s)
         conv = q.ck[0:1, :] * q.PR[s, pl.ds(8, T)]
         conv = conv + q.ck[1:2, :] * q.PR[s, pl.ds(7, T)] * m1
         conv = conv + q.ck[2:3, :] * q.PR[s, pl.ds(6, T)] * m2
         q.CO[s] = conv
-        gated = (q.GCV[s] * conv).astype(BF)
-        q.GATED[s] = gated
-        put_part("R1", q.SB, q.OWN, e, dot(gated, q.OUTW[...]))
+        q.GF[c, pl.ds(pl.multiple_of(s * T, T), T)] = (q.GCV[s] * conv).astype(BF)
         return carry
 
-    lax.fori_loop(0, 4, conv_step, 0)
+    lax.fori_loop(0, 2, conv_step, 0)
+    gather_start("GF", (0, 3))
+    lax.fori_loop(2, 4, conv_step, 0)
+    gather_start("GF", (1, 2))
+    gather_start("COT")
     weight_forward(2)
+    out_stage_core()
+    gather_pass("GF")
     weight_forward(3)
-
-    hidden = q.X[...].astype(F32) + reduce_sum("R1", q.SB, q.OWN)
-    q.HID[...] = hidden
-    q.N2[c] = (hidden * norm_scale(hidden) * q.GA[1:2, :]).astype(BF)
-    gather_start("N2")
+    for d in (1, 3, 2):
+        gather_take("GF", d)
+    gather_pass("COT")
+    out_ready()
+    weight_ready(2)
+    weight_ready(3)
     for d in (1, 3, 2):
         gather_take("COT", d)
-    gather_end("COT")
-    weight_ready(2)
-    weight_ready(3)
 
     def ffn_step(i, carry):
-        d = arrival(i)
-        s = mod(c - d, 4)
-        e = mod(4 - d, 4)
-
-        @pl.when(i > 0)
-        def _():
-            gather_take("N2", d)
-
+        e = far_first(i)
+        s = mod(c + e, 4)
+        at = pl.ds(pl.multiple_of(s * T, T), T)
+        gated = jnp.concatenate([q.GF[n, at] for n in range(4)], axis=1)
+        hidden = q.XF[s].astype(F32) + dot(gated, q.OUTF[...].reshape(D, D))
+
+        @pl.when(e == 0)
+        def _():
+            q.HID[...] = hidden
+
+        q.N2[s] = (hidden * norm_scale(hidden) * q.GA[1:2, :]).astype(BF)
         rows = q.N2[s]
         gate = dot(rows, q.GUW[0])
         up = dot(rows, q.GUW[1])
@@ -414,11 +516,12 @@
         q.GG[s, :, 0:H] = (ga * up * sig * (1.0 + gate * (1.0 - sig))).astype(BF)
         q.GG[s, :, H:] = (ga * silu).astype(BF)
         part = dot_nt(q.GG[s, :, 0:H], q.GUW[0]) + dot_nt(q.GG[s, :, H:], q.GUW[1])
-        put_part("R2", q.SB, q.OWN, e, part)
+        put_part("R2", q.OWN, e, part)
         return carry
 
     lax.fori_loop(0, 4, ffn_step, 0)
-    gather_end("N2")
+    gather_end("GF")
+    gather_end("COT")
 
     def unit(name):
         return next(u for u in UNITS if u[0] == name)
@@ -568,7 +671,7 @@
     def grad_out_in(core):
         def step(a, carry):
             rows = features(q.N1, a, core)
-            gated = q.GATED[...].reshape(4 * T, W)
+            gated = q.GF[c]
             q.oi0_W[core, pl.ds(2 * a, 2), :, :, 0:W] = dot_tn(gated, features(q.GB, a, core)).astype(BF).reshape(2, 4, 32, W)
             into = dot_tn(rows, q.GM[...].reshape(4 * T, 3 * W)).astype(BF).reshape(2, 4, 32, 3 * W)
             q.oi0_W[core, pl.ds(2 * a, 2), :, :, W:] = into[:, :, :, 0:W]
@@ -576,6 +679,12 @@
             return carry
 
         lax.fori_loop(0, 2, step, 0)
+
+    def norm_back(value, scale, gain, grad):
+        weighted = grad * gain
+        inner = jnp.sum(weighted * value, axis=1, keepdims=True)
+        back = scale * weighted - value * (scale * scale * scale) * inner / D
+        return back, jnp.sum(grad * value * scale, axis=0, keepdims=True)
 
     grad_down(1 - k)
     core_send("dn0")
@@ -584,14 +693,9 @@
     core_send("gt")
     core_send("up")
     grad_down(k)
-
-    def norm_back(value, scale, gain, grad):
-        weighted = grad * gain
-        inner = jnp.sum(weighted * value, axis=1, keepdims=True)
-        back = scale * weighted - value * (scale * scale * scale) * inner / D
-        return back, jnp.sum(grad * value * scale, axis=0, keepdims=True)
-
-    grad_normed = reduce_sum("R2", q.SB, q.OWN)
+    stage_one("dn0")
+    stage_one("dn1")
+    grad_normed = reduce_sum("R2", q.OWN)
     hidden = q.HID[...]
     back, grad_gain = norm_back(hidden, norm_scale(hidden), q.GA[1:2, :], grad_normed)
     q.SM[...] = jnp.zeros((8, D), F32)
@@ -599,10 +703,18 @@
     grad_hidden = q.COT[c].astype(F32) + back
     q.GB[c] = grad_hidden.astype(BF)
     q.OWN[...] = grad_hidden
+    grad_gated = dot_nt(q.GB[c], q.OUTF[...].reshape(D, D)).astype(BF)
+    for n in range(4):
+        q.GGS[n] = grad_gated[:, n * W : (n + 1) * W]
+
+    def gated_copy(d, dst):
+        return rcopy(q.GGS.at[mod(c + d, 4)], q.GGR.at[dst], q.GG_s.at[d], q.GG_r.at[d], at_z(d))
+
+    for d in (1, 3, 2):
+        gated_copy(d, c).start()
     gather_start("GB")
+    q.GGR[c] = q.GGS[c]
     grad_gate_up(k)
-    stage_one("dn0")
-    stage_one("dn1")
     stage_one("gt")
     stage_one("up")
 
@@ -611,15 +723,12 @@
         q.FM[0, 4, pl.ds(T, 8)] = jnp.zeros((8, W), F32)
         q.FM[1, 4, pl.ds(T, 8)] = jnp.zeros((8, W), F32)
 
-    def conv_back_step(i, carry):
-        d = arrival(i)
-        s = mod(c - d, 4)
-
-        @pl.when(i > 0)
-        def _():
-            gather_take("GB", d)
-
-        grad_gated = dot_nt(q.GB[s], q.OUTW[...])
+    for d in (1, 3, 2):
+        gated_copy(d, c).wait_send()
+        gated_copy(d, mod(c - d, 4)).wait_recv()
+
+    def conv_back_step(s, carry):
+        grad_gated = q.GGR[s].astype(F32)
         q.GM[s, :, W : 2 * W] = (grad_gated * q.CO[s]).astype(BF)
         grad_conv = grad_gated * q.GCV[s]
         q.GCONV[s] = grad_conv
@@ -629,10 +738,10 @@
         return carry
 
     lax.fori_loop(0, 4, conv_back_step, 0)
-    gather_end("GB")
     halo_b = rcopy(q.FM.at[:, 1:5, 0:8], q.FM.at[:, pl.ds(k, 4), pl.ds(T, 8)], q.halo.at[2], q.halo.at[3], mate)
     halo_bt = rcopy(q.FM.at[:, 1:5, 0:8], q.FM.at[:, pl.ds(1 - k, 4), pl.ds(T, 8)], q.halo.at[2], q.halo.at[3], mate)
     halo_b.start()
+    gather_pass("GB")
     halo_b.wait_send()
     halo_bt.wait_recv()
 
@@ -649,26 +758,29 @@
         q.GM[s, :, 0:W] = (grad_product * q.VAL[s]).astype(BF)
         q.GM[s, :, 2 * W :] = (grad_product * q.GBV[s]).astype(BF)
         part = dot_nt(q.GM[s, :, 0:W], q.INW[0]) + dot_nt(q.GM[s, :, W : 2 * W], q.INW[1]) + dot_nt(q.GM[s, :, 2 * W :], q.INW[2])
-        put_part("R3", q.SB, q.OWNF, e, part)
+        put_part("R3", q.OWNF, e, part)
         return carry
 
     lax.fori_loop(0, 4, product_back_step, 0)
+    for d in (1, 3, 2):
+        gather_take("GB", d)
     grad_out_in(1 - k)
     core_send("oi0")
     core_send("oi1")
     grad_out_in(k)
-
-    grad_normed = reduce_sum("R3", q.SB, q.OWNF)
+    gather_end("GB")
+    stage_two("dn0")
+    stage_two("dn1")
+    stage_one("oi0")
+    stage_one("oi1")
+
+    grad_normed = reduce_sum("R3", q.OWNF)
 
     def ffn_out_step(i, carry):
         e = far_first(i)
         s = mod(c + e, 4)
-        put_part("RF", q.SBF, q.OWNF, e, dot(q.A[s], q.DNW[...]))
+        put_part("RF", q.OWNF, e, dot(q.A[s], q.DNW[...]))
         return carry
-
-    lax.fori_loop(0, 4, ffn_out_step, 0)
-    stage_one("oi0")
-    stage_one("oi1")
 
     def home(n):
         buf, out = ((q.MIXB, q.o_mixed), (q.GTB, q.o_gt))[n]
@@ -709,7 +821,7 @@
 
         away.wait_send()
 
-    inputs = q.X[...].astype(F32)
+    inputs = q.XF[c].astype(F32)
     back, grad_gain = norm_back(inputs, norm_scale(inputs), q.GA[0:1, :], grad_normed)
     q.SM[0:1, :] = grad_gain
     q.GTB[...] = (q.OWN[...] + back).astype(BF)
@@ -717,8 +829,11 @@
 
     small_core = rcopy(q.SM, q.SMC, q.SM_s.at[0], q.SM_r.at[0], mate)
     small_core.start()
-    for name in ("dn0", "dn1", "gt", "up"):
-        stage_two(name)
+    lax.fori_loop(0, 4, ffn_out_step, 0)
+    stage_two("gt")
+    stage_two("up")
+    stage_three("dn0")
+    stage_three("dn1")
     small_core.wait()
 
     def small_step(buf, me, base, target, value, rows):
@@ -734,24 +849,28 @@
         return (buf[0] + buf[1]) + (buf[2] + buf[3])
 
     small_step(q.SMX, x, 1, at_x, q.SM[...] + q.SMC[...], 8)
-    for name in ("dn0", "dn1", "gt", "up"):
-        stage_three(name)
     stage_two("oi0")
     stage_two("oi1")
+    stage_three("gt")
+    stage_three("up")
+    stage_four("dn0")
+    stage_four("dn1")
     total = small_take(q.SMX, x, 1, at_x)
     small_step(q.SMY, y, 4, at_y, total, 8)
-    q.MIXB[...] = (q.HID[...] + reduce_sum("RF", q.SBF, q.OWNF)).astype(BF)
+    q.MIXB[...] = (q.HID[...] + reduce_sum("RF", q.OWNF)).astype(BF)
     home_start(0)
-    for name in ("dn0", "dn1", "gt", "up"):
-        stage_four(name)
+    stage_four("gt")
+    stage_four("up")
     stage_three("oi0")
     stage_three("oi1")
     total = small_take(q.SMY, y, 4, at_y)
     small_step(q.SMZ, c, 7, at_z, total, 8)
+    stage_five("dn0")
+    stage_five("dn1")
     stage_four("oi0")
     stage_four("oi1")
-    for name in ("dn0", "dn1", "gt", "up"):
-        stage_five(name)
+    stage_five("gt")
+    stage_five("up")
     q.o_small[...] = total
     total = small_take(q.SMZ, c, 7, at_z)
     q.o_small[0:2, :] = total[0:2, :]
@@ -760,7 +879,7 @@
     home_wait(0)
     home_wait(1)
     gain_send.wait_send()
-    for w in range(4):
+    for w in (0, 2, 3):
         weight_end(w)
     for name in ("dn0", "dn1", "gt", "up", "oi0", "oi1"):
         stage_six(name)

time: 179 us -> 156 us (0.87)
  Pallas kernels: 162 us -> 140 us
    pallas_call x1, Pallas kernels: 162 us -> 140 us  [per_device(): pl.pallas_call(kernel, out_shape=(jax.ShapeDtypeStruct((2 * T, HALF), BF)...]
where the time goes in v2:
time: 156 us
  Pallas kernels  140 us (90%)
  other arithmetic  11.2 us (7%)
  local copies, waits for them, and re-layouts  4.34 us (3%)
    pallas_call x1, Pallas kernels, per_device(): pl.pallas_call(kernel, out_shape=(jax.ShapeDtypeStruct((2 * T, HALF), BF)...  140 us
    convert_element_type x1, other arithmetic, per_device(): g_gu.reshape(2, HALF, H).astype(F32)  4.25 us

profile of v2, /device:TPU:1, one launch (start us, length us, event | category | flops | bytes accessed | tf_op | source)
XLA Modules:
  0.0 155.9 jit_solution(6104689876176126384)
XLA Ops:
  0.6 0.7 convert_element_type.30
  1.3 0.8 broadcast_in_dim.17.refs_2_
  2.1 0.1 pad.2.clone
  2.2 1.4 maximum_maximum_fusion.refs_3_
  3.6 139.7 %block_step.1 = (bf16[256,512]{1,0:T(8,128)(2,1)}, bf16[256,512]{1,0:T(8,128)(2,1)}, f32[8,1024]{1,0:T(8,128)}, bf16[3,2,2,4,32,256]{5,4,3,2,1,0:T(8,128)(2,1)},...) custom-call(bf16[256,512]{1,0:T(8,128)(2,1)} %refs_0_.1, ...), custom_call_target="tpu_custom_call" | custom-call | tf_op jit(solution)/shard_map/block_step/pallas_call | solution.py:904
  143.3 1.5 fusion
  144.7 1.3 slice.10
  146.0 0.0 copy-start
  146.0 4.3 %bitcast_convert_fusion = f32[2,512,1152]{2,1,0:T(8,128)} fusion(bf16[2,2,2,4,32,1152]{5,4,3,2,1,0:T(8,128)(2,1)} %get-tuple-element.21), kind=kLoop, calls=%fused_computation | loop fusion | flops 1179648 | bytes 7077888 | tf_op jit(solution)/shard_map/convert_element_type | solution.py:932
  150.3 0.0 copy-start.1
  150.3 0.0 copy-done
  150.3 0.0 copy-start.3
  150.3 1.8 %bitcast_convert_fusion.1 = f32[1152,512]{1,0:T(8,128)} fusion(bf16[2,4,144,512]{3,2,1,0:T(8,128)(2,1)S(1)} %copy-done), kind=kLoop, calls=%fused_computation.1 | loop fusion | flops 589824 | bytes 3538944 | tf_op jit(solution)/shard_map/convert_element_type | solution.py:933
  152.1 0.0 copy-start.2
  152.1 0.0 copy-start.4
  152.1 0.0 copy-done.1
  152.1 1.3 bitcast_convert_fusion.2
  153.4 0.0 copy-done.3
  153.4 0.9 bitcast_convert_fusion.3
  154.3 0.0 copy-done.2
  154.3 0.9 convert_element_type.31
  155.2 0.0 copy-done.4
  155.2 0.7 copy.20
  (1 shorter events, 0.0 us)
Async XLA Ops:
  146.0 4.3 %copy-start = (bf16[2,4,144,512]{3,2,1,0:T(8,128)(2,1)S(1)}, bf16[2,4,144,512]{3,2,1,0:T(8,128)(2,1)}, u32[]{:S(2)}) copy-start(bf16[2,4,144,512]{3,2,1,0:T(8,128)(2,1)} %get-tuple-element.22) | copy-start | bytes 3538948
  150.3 1.8 %copy-start.1 = (bf16[3,2,2,4,32,256]{5,4,3,2,1,0:T(8,128)(2,1)S(1)}, bf16[3,2,2,4,32,256]{5,4,3,2,1,0:T(8,128)(2,1)}, u32[]{:S(2)}) copy-start(bf16[3,2,2,4,32,256]{5,4,3,2,1,0:T(8,128)(2,1)} %get-tuple-element.19) | copy-start | bytes 2359300
  150.3 3.1 %copy-start.3 = (bf16[2,4,32,512]{3,2,1,0:T(8,128)(2,1)S(1)}, bf16[2,4,32,512]{3,2,1,0:T(8,128)(2,1)}, u32[]{:S(2)}) copy-start(bf16[2,4,32,512]{3,2,1,0:T(8,128)(2,1)} %get-tuple-element.20) | copy-start | bytes 786436
  152.1 2.2 %copy-start.2 = (bf16[256,512]{1,0:T(8,128)(2,1)S(1)}, bf16[256,512]{1,0:T(8,128)(2,1)}, u32[]{:S(2)}) copy-start(bf16[256,512]{1,0:T(8,128)(2,1)} %get-tuple-element.17) | copy-start | bytes 786436
  152.1 3.1 %copy-start.4 = (bf16[256,512]{1,0:T(8,128)(2,1)S(1)}, bf16[256,512]{1,0:T(8,128)(2,1)}, u32[]{:S(2)}) copy-start(bf16[256,512]{1,0:T(8,128)(2,1)} %get-tuple-element.34) | copy-start | bytes 786436

commit v3 on v2

--- a/solution.py
+++ b/solution.py
@@ -48,7 +48,14 @@
     s["o_s"] = dma((8,))
     s["o_r"] = dma((8,))
     s["o_l"] = dma((1,))
-    v("GUW", (2, D, H), BF)
+    v("GUW", (2, 2, 4, 2, 64, H), BF)
+    s["gu_s"] = dma((3,))
+    s["gu_r"] = dma((3,))
+    for n in ("GUX", "OUX"):
+        s[n + "_s"] = dma((6,))
+        s[n + "_r"] = dma((6,))
+    v("REACH", (2, 2, T, 128), BF)
+    v("GAINS", (8, HALF), F32)
     v("DNW", (H, D), BF)
     v("M", (4, T, 128), BF)
     v("GA", (8, D), F32)
@@ -66,12 +73,13 @@
     for n in ("GBV", "GCV", "VAL", "CO", "GCONV"):
         v(n, (4, T, W), F32)
     v("FM", (2, 5, T + 8, W), F32)
-    v("HID", (T, D), F32)
+    v("HID", (4, T, D), F32)
     v("A", (4, T, H), BF)
     v("GG", (4, T, 2 * H), BF)
     v("GM", (4, T, 3 * W), BF)
     v("OWN", (T, D), F32)
     v("OWNF", (T, D), F32)
+    v("OWNB", (T, D), F32)
     for n in ("R2", "R3", "RF"):
         v(n, (2, T, D), BF)
         v(n + "_T", (2, T // 2, D), BF)
@@ -81,12 +89,13 @@
     v("MIXB", (T, D), BF)
     v("GTB", (T, D), BF)
     v("SM", (8, D), F32)
-    v("SMC", (8, D), F32)
-    v("SMX", (4, 8, D), F32)
-    v("SMY", (4, 8, D), F32)
-    v("SMZ", (4, 8, D), F32)
-    s["SM_s"] = dma((12,))
-    s["SM_r"] = dma((12,))
+    for n, rows in (("SE", 16), ("SL", 8)):
+        v(n, (rows, 128), F32)
+        v(n + "C", (rows, 128), F32)
+        for axis in "XYZ":
+            v(n + axis, (4, rows, 128), F32)
+        s[n + "_s"] = dma((10,))
+        s[n + "_r"] = dma((10,))
     s["sw_s"] = dma((10,))
     s["sw_r"] = dma((10,))
     s["ga"] = dma((3,))
@@ -97,17 +106,18 @@
     for n, m, k, _ in UNITS:
         v(n + "_W", (2, 4, 4, m, k), BF)
         v(n + "_C", (4, 4, m, k), BF)
-        v(n + "_R1", (3, 4, m, k), BF)
+        v(n + "_R1", (2, 4, m, k), BF)
+        v(n + "_T", (2, 2, m, k), BF)
         v(n + "_S", (4, m, k), BF)
         v(n + "_R2", (3, m, k), BF)
         v(n + "_O", (2, 4, m, k), BF)
-        s[n + "_s"] = dma((14,))
-        s[n + "_r"] = dma((14,))
+        s[n + "_s"] = dma((8,))
+        s[n + "_r"] = dma((19,))
         s[n + "_l"] = dma((2,))
     return s
 
 
-IN_NAMES = ("tok", "cot", "reach", "gains", "ck", "inw", "outw", "guw", "dnw")
+IN_NAMES = ("tok", "cot", "reach", "mgain", "fgain", "ck", "inw", "outw", "guw", "dnw")
 OUT_NAMES = ("o_mixed", "o_gt", "o_small", "o_in", "o_out", "o_gu", "o_dn")
 
 
@@ -163,13 +173,17 @@
     friends += [f(d) for f in (at_x, at_y, at_z) for d in (1, 2, 3)]
     for to in friends:
         pl.semaphore_signal(barrier, inc=1, device_id=to, device_id_type=MESH)
+
+    for n in range(4):
+        q.REACH[n // 2, n % 2] = jnp.broadcast_to(q.reach[n : n + 1, :].astype(F32), (T, 128)).T.astype(BF)
+    q.GAINS[...] = jnp.zeros((8, HALF), F32)
+    q.GAINS[0:1, :] = q.mgain[...]
+    q.GAINS[1:2, :] = q.fgain[...]
     pl.semaphore_wait(barrier, len(friends))
 
     def weight_regions(w):
         if w == 0:
             return (q.inw, q.INW, lambda p, n, a: (q.inw.at[:, pl.ds(p * 128, 128 * n), :], q.INW.at[:, pl.ds(a * HALF + p * 128, 128 * n), :]))
-        if w == 2:
-            return (q.guw, q.GUW, lambda p, n, a: (q.guw.at[:, pl.ds(p * 128, 128 * n), :], q.GUW.at[:, pl.ds(a * HALF + p * 128, 128 * n), :]))
         return (q.dnw, q.DNW, lambda p, n, a: (q.dnw.at[pl.ds(p * 288, 288 * n), :], q.DNW.at[pl.ds(p * 288, 288 * n), pl.ds(pl.multiple_of(a * HALF, HALF), HALF)]))
 
     def weight_local(w):
@@ -211,8 +225,20 @@
             weight_send(w, s).wait_send()
         weight_pass(w, k).wait_send()
 
-    for w in (0, 2, 3):
+    for w in (0, 3):
         weight_local(w).start()
+
+    gu_local = pltpu.make_async_copy(q.guw, q.GUW.at[:, r], q.w_l.at[2])
+
+    def gu_row(s, a):
+        h = pl.ds(s * 32, 32)
+        return rcopy(q.guw.at[:, x, k, h], q.GUW.at[:, a, x, k, h], q.gu_s.at[s], q.gu_r.at[s], at_y(1 - 2 * s))
+
+    def gu_core(core):
+        view = q.GUW.at[:, 1 - r, :, core]
+        return rcopy(view, view, q.gu_s.at[2], q.gu_r.at[2], mate)
+
+    gu_local.start()
 
     half = lambda a: pl.ds(pl.multiple_of(a * HALF, HALF), HALF)
     out_own = q.outw.at[pl.ds(x * 64 + k * 32, 32), :]
@@ -224,10 +250,6 @@
     def out_col(d, a):
         view = q.OUTF.at[a, x, k]
         return rcopy(view, view, q.o_s.at[d], q.o_r.at[d], at_z(d))
-
-    def out_x(d, a):
-        view = q.OUTF.at[:, a, k]
-        return rcopy(view, view, q.o_s.at[3 + d], q.o_r.at[3 + d], at_x(d))
 
     def out_core(core):
         view = q.OUTF.at[:, :, core]
@@ -239,30 +261,27 @@
         for d in (1, 3, 2):
             out_col(d, c).start()
 
-    def out_stage_x():
-        for d in (1, 3, 2):
-            out_col(d, mod(c - d, 4)).wait_recv()
-        for d in (1, 3, 2):
-            out_x(d, x).start()
-
-    def out_stage_core():
-        for d in (1, 3, 2):
-            out_x(d, mod(x - d, 4)).wait_recv()
-        out_core(k).start()
-
     def out_ready():
         out_core(1 - k).wait_recv()
         out_row(r).wait_send()
         for d in (1, 2, 3):
             out_col(d, c).wait_send()
-            out_x(d, x).wait_send()
+        ring_end(OUX)
         out_core(k).wait_send()
+
+    def gu_ready():
+        gu_local.wait()
+        gu_core(1 - k).wait_recv()
+        for n in (0, 1):
+            gu_row(n, r).wait_send()
+        ring_end(GUX)
+        gu_core(k).wait_send()
 
     def swap_views(n):
         if n == 0:
             return lambda j: q.tok.at[pl.ds(j * T, T), :], lambda a: q.XF.at[c, :, pl.ds(pl.multiple_of(a * HALF, HALF), HALF)]
         if n == 1:
-            return lambda j: q.reach.at[:, j], lambda a: q.M.at[pl.ds(2 * a, 2)]
+            return lambda j: q.REACH.at[:, j], lambda a: q.M.at[pl.ds(2 * a, 2)]
         return lambda j: q.cot.at[pl.ds(j * T, T), :], lambda a: q.COT.at[c, :, pl.ds(pl.multiple_of(a * HALF, HALF), HALF)]
 
     def swap_near(n):
@@ -308,9 +327,9 @@
     def gain_view(a):
         return q.GA.at[:, pl.ds(pl.multiple_of(a * HALF, HALF), HALF)]
 
-    gain_local = pltpu.make_async_copy(q.gains, gain_view(r), q.ga.at[0])
-    gain_send = rcopy(q.gains, gain_view(r), q.ga.at[1], q.ga.at[2], dev(r_=1 - r))
-    gain_take = rcopy(q.gains, gain_view(1 - r), q.ga.at[1], q.ga.at[2], dev(r_=1 - r))
+    gain_local = pltpu.make_async_copy(q.GAINS, gain_view(r), q.ga.at[0])
+    gain_send = rcopy(q.GAINS, gain_view(r), q.ga.at[1], q.ga.at[2], dev(r_=1 - r))
+    gain_take = rcopy(q.GAINS, gain_view(1 - r), q.ga.at[1], q.ga.at[2], dev(r_=1 - r))
 
     swap_start(0)
     gain_local.start()
@@ -320,46 +339,51 @@
     weight_start(0)
     swap_start(1)
 
-    def gather(name, n, a):
-        buf = getattr(q, name)
+    class Ring:
+        def __init__(self, name, view, me, target, first=0):
+            self.name, self.view, self.me, self.target, self.first = name, view, me, target, first
+
+        def copy(self, n, a):
+            view = self.view(a, (0, 1, 1, 0, 0, 1)[n])
+            sends, takes = getattr(q, self.name + "_s"), getattr(q, self.name + "_r")
+            return rcopy(view, view, sends.at[n], takes.at[self.first + n], self.target(3 if n in (1, 3, 5) else 1))
+
+    def col_view(buf):
         rows = buf.shape[1] // 2
-        h = (0, 1, 1, 0, 0, 1)[n]
-        view = buf.at[a, pl.ds(h * rows, rows)]
-        return rcopy(view, view, getattr(q, name + "_s").at[n], getattr(q, name + "_r").at[n], at_z(3 if n in (1, 3, 5) else 1))
-
-    def gather_start(name, parts=(0, 1, 2, 3)):
+        return lambda a, h: buf.at[a, pl.ds(h * rows, rows)]
+
+    XF = Ring("XF", col_view(q.XF), c, at_z)
+    COT = Ring("COT", col_view(q.COT), c, at_z)
+    GF = Ring("GF", col_view(q.GF), c, at_z)
+    GB = Ring("GB", col_view(q.GB), c, at_z)
+    GUX = Ring("GUX", lambda a, h: q.GUW.at[:, 1 - r, a, k, pl.ds(h * 32, 32)], x, at_x)
+    OUX = Ring("OUX", lambda a, h: q.OUTF.at[:, a, k, pl.ds(h * 16, 16)], x, at_x)
+
+    def ring_start(ring, parts=(0, 1, 2, 3)):
         for n in parts:
-            gather(name, n, c).start()
-
-    def gather_pass(name):
-        gather(name, 0, mod(c - 1, 4)).wait_recv()
-        gather(name, 4, mod(c - 1, 4)).start()
-        gather(name, 1, mod(c + 1, 4)).wait_recv()
-        gather(name, 5, mod(c + 1, 4)).start()
-
-    def gather_take(name, d):
+            ring.copy(n, ring.me).start()
+
+    def ring_pass(ring):
+        before, after = mod(ring.me - 1, 4), mod(ring.me + 1, 4)
+        ring.copy(0, before).wait_recv()
+        ring.copy(4, before).start()
+        ring.copy(1, after).wait_recv()
+        ring.copy(5, after).start()
+
+    def ring_take(ring, d):
         if d == 1:
-            gather(name, 2, mod(c - 1, 4)).wait_recv()
+            ring.copy(2, mod(ring.me - 1, 4)).wait_recv()
         elif d == 3:
-            gather(name, 3, mod(c + 1, 4)).wait_recv()
+            ring.copy(3, mod(ring.me + 1, 4)).wait_recv()
         else:
-            gather(name, 4, mod(c + 2, 4)).wait_recv()
-            gather(name, 5, mod(c + 2, 4)).wait_recv()
-
-    def gather_step(name, i):
-        for n, d in ((1, 1), (2, 3), (3, 2)):
-
-            @pl.when(i == n)
-            def _():
-                if n == 1:
-                    gather_pass(name)
-                gather_take(name, d)
-
-    def gather_end(name):
+            ring.copy(4, mod(ring.me + 2, 4)).wait_recv()
+            ring.copy(5, mod(ring.me + 2, 4)).wait_recv()
+
+    def ring_end(ring):
         for n in (0, 1, 2, 3):
-            gather(name, n, c).wait_send()
-        gather(name, 4, mod(c - 1, 4)).wait_send()
-        gather(name, 5, mod(c + 1, 4)).wait_send()
+            ring.copy(n, ring.me).wait_send()
+        ring.copy(4, mod(ring.me - 1, 4)).wait_send()
+        ring.copy(5, mod(ring.me + 1, 4)).wait_send()
 
     HT = T // 2
 
@@ -385,48 +409,48 @@
 
     def put_part(name, own, e, part):
         mid, send = getattr(q, name + "_T"), getattr(q, name + "_B")
-
-        @pl.when(e == 0)
-        def _():
+        if e == 0:
             own[...] = part
-
-        @pl.when(e == 2)
-        def _():
+        elif e == 2:
             send[1] = part.astype(BF)
             reduce_copy(name, 0).start()
             reduce_copy(name, 1).start()
-
-        @pl.when(e == 1)
-        def _():
+        elif e == 1:
             send[0, HT:T] = part[HT:].astype(BF)
             reduce_copy(name, 2).start()
             reduce_copy(name, 0).wait_recv()
             send[0, 0:HT] = (part[:HT] + mid[0].astype(F32)).astype(BF)
             reduce_copy(name, 3).start()
-
-        @pl.when(e == 3)
-        def _():
+        else:
             send[2, 0:HT] = part[:HT].astype(BF)
             reduce_copy(name, 4).start()
             reduce_copy(name, 1).wait_recv()
             send[2, HT:T] = (part[HT:] + mid[1].astype(F32)).astype(BF)
             reduce_copy(name, 5).start()
 
+    def two_chunks(ref, pair, lanes=slice(None)):
+        return jnp.concatenate([ref[mod(c + e, 4), :, lanes] for e in pair], axis=0)
+
+    def put_pair(name, own, pair, part):
+        for n, e in enumerate(pair):
+            put_part(name, own, e, part[n * T : (n + 1) * T])
+
     def arrival(i):
         return i + lax.div(i, 2) - 2 * lax.div(i, 3)
 
-    def far_first(i):
-        return mod(2 - i + 3 * lax.div(i, 2) - 2 * lax.div(i, 3), 4)
-
     def norm_scale(value):
         return lax.rsqrt(jnp.sum(value * value, axis=1, keepdims=True) / D + EPS)
 
     swap_wait(0)
-    gather_start("XF")
+    ring_start(XF)
+    for n in (0, 1):
+        gu_row(n, r).start()
     swap_start(2)
-    for w in (2, 3):
-        weight_start(w)
-    out_stage_col()
+    out_local.wait()
+    out_row(1 - r).wait_recv()
+    for d in (1, 3, 2):
+        out_col(d, c).start()
+    weight_start(3)
     gain_local.wait()
     gain_take.wait_recv()
     weight_forward(0)
@@ -438,7 +462,26 @@
 
     def in_step(i, carry):
         s = mod(c - arrival(i), 4)
-        gather_step("XF", i)
+
+        @pl.when(i == 1)
+        def _():
+            ring_pass(XF)
+            ring_take(XF, 1)
+
+        @pl.when(i == 2)
+        def _():
+            for d in (1, 3, 2):
+                out_col(d, mod(c - d, 4)).wait_recv()
+            ring_start(OUX)
+            ring_take(XF, 3)
+
+        @pl.when(i == 3)
+        def _():
+            for n in (0, 1):
+                gu_row(n, 1 - r).wait_recv()
+            ring_start(GUX)
+            ring_take(XF, 2)
+
         inputs = q.XF[s].astype(F32)
         q.N1[s] = (inputs * norm_scale(inputs) * q.GA[0:1, :]).astype(BF)
         rows = q.N1[s]
@@ -454,9 +497,6 @@
     halo_f = rcopy(q.PR.at[0:4, pl.ds(T, 8)], q.PR.at[pl.ds(k, 4), 0:8], q.halo.at[0], q.halo.at[1], mate)
     halo_ft = rcopy(q.PR.at[0:4, pl.ds(T, 8)], q.PR.at[pl.ds(1 - k, 4), 0:8], q.halo.at[0], q.halo.at[1], mate)
     halo_f.start()
-    gather_end("XF")
-    out_stage_x()
-    swap_wait(2)
     swap_wait(1)
     halo_f.wait_send()
     halo_ft.wait_recv()
@@ -477,51 +517,55 @@
         return carry
 
     lax.fori_loop(0, 2, conv_step, 0)
-    gather_start("GF", (0, 3))
+    ring_start(GF, (0, 3))
     lax.fori_loop(2, 4, conv_step, 0)
-    gather_start("GF", (1, 2))
-    gather_start("COT")
-    weight_forward(2)
-    out_stage_core()
-    gather_pass("GF")
+    ring_start(GF, (1, 2))
+    ring_pass(OUX)
+    ring_pass(GUX)
+    ring_pass(GF)
+    swap_wait(2)
+    ring_start(COT)
+    for d in (1, 3, 2):
+        ring_take(OUX, d)
+    out_core(k).start()
     weight_forward(3)
     for d in (1, 3, 2):
-        gather_take("GF", d)
-    gather_pass("COT")
+        ring_take(GUX, d)
+    gu_core(k).start()
+    for d in (1, 3, 2):
+        ring_take(GF, d)
     out_ready()
-    weight_ready(2)
+    gu_ready()
     weight_ready(3)
-    for d in (1, 3, 2):
-        gather_take("COT", d)
-
-    def ffn_step(i, carry):
-        e = far_first(i)
-        s = mod(c + e, 4)
-        at = pl.ds(pl.multiple_of(s * T, T), T)
-        gated = jnp.concatenate([q.GF[n, at] for n in range(4)], axis=1)
-        hidden = q.XF[s].astype(F32) + dot(gated, q.OUTF[...].reshape(D, D))
-
-        @pl.when(e == 0)
-        def _():
-            q.HID[...] = hidden
-
+
+    def out_step(n, carry):
+        lanes = pl.ds(pl.multiple_of(n * HALF, HALF), HALF)
+        gated = jnp.concatenate([q.GF[m] for m in range(4)], axis=1)
+        branch = dot(gated, q.OUTF[:, :, :, :, lanes].reshape(D, HALF))
+        q.HID[:, :, lanes] = q.XF[:, :, lanes].astype(F32) + branch.reshape(4, T, HALF)
+        return carry
+
+    lax.fori_loop(0, 2, out_step, 0)
+
+    def norm_step(s, carry):
+        hidden = q.HID[s]
         q.N2[s] = (hidden * norm_scale(hidden) * q.GA[1:2, :]).astype(BF)
-        rows = q.N2[s]
-        gate = dot(rows, q.GUW[0])
-        up = dot(rows, q.GUW[1])
+        return carry
+
+    lax.fori_loop(0, 4, norm_step, 0)
+
+    COLS = ((0, 512), (512, 512), (1024, 128))
+    for at, n in COLS:
+        rows = q.N2[...].reshape(4 * T, D)
+        gate = dot(rows, q.GUW[0, :, :, :, :, at : at + n].reshape(D, n))
+        up = dot(rows, q.GUW[1, :, :, :, :, at : at + n].reshape(D, n))
         sig = 1.0 / (1.0 + jnp.exp(-gate))
         silu = gate * sig
-        q.A[s] = (silu * up).astype(BF)
-        ga = dot_nt(q.COT[s], q.DNW[...])
-        q.GG[s, :, 0:H] = (ga * up * sig * (1.0 + gate * (1.0 - sig))).astype(BF)
-        q.GG[s, :, H:] = (ga * silu).astype(BF)
-        part = dot_nt(q.GG[s, :, 0:H], q.GUW[0]) + dot_nt(q.GG[s, :, H:], q.GUW[1])
-        put_part("R2", q.OWN, e, part)
-        return carry
-
-    lax.fori_loop(0, 4, ffn_step, 0)
-    gather_end("GF")
-    gather_end("COT")
+        q.A[:, :, at : at + n] = (silu * up).astype(BF).reshape(4, T, n)
+        q.GG[:, :, at : at + n] = (up * sig * (1.0 + gate * (1.0 - sig))).astype(BF).reshape(4, T, n)
+        q.GG[:, :, H + at : H + at + n] = silu.astype(BF).reshape(4, T, n)
+        if at == 0:
+            ring_pass(COT)
 
     def unit(name):
         return next(u for u in UNITS if u[0] == name)
@@ -530,32 +574,41 @@
         return getattr(q, name + "_" + what)
 
     def core_copy(name, core):
-        return rcopy(g(name, "W").at[core], g(name, "C"), g(name, "s").at[0], g(name, "r").at[0], mate)
-
-    def first_copy(name, d):
+        return rcopy(g(name, "W").at[core], g(name, "C"), g(name, "s").at[7], g(name, "r").at[0], mate)
+
+    def first_view(name, d, h):
         w = g(name, "W")
         if unit(name)[3] == 0:
-            src, to = w.at[k, :, mod(x + d, 4)], at_x(d)
+            return w.at[k, pl.ds(2 * h, 2), mod(x + d, 4)]
+        return w.at[k, slot_y(d), pl.ds(2 * h, 2)]
+
+    def first_copy(name, n):
+        e, h, d = ((2, 0, 1), (2, 1, 3), (1, 1, 1), (1, 0, 1), (3, 0, 3), (3, 1, 3))[n]
+        if n < 2:
+            dst = g(name, "T").at[h]
         else:
-            src, to = w.at[k, slot_y(d)], at_y(d)
-        return rcopy(src, g(name, "R1").at[d - 1], g(name, "s").at[d], g(name, "r").at[d], to)
+            dst = g(name, "R1").at[e // 2, pl.ds(2 * h, 2)]
+        to = at_x(d) if unit(name)[3] == 0 else at_y(d)
+        return rcopy(first_view(name, e, h), dst, g(name, "s").at[n], g(name, "r").at[1 + n], to)
 
     def second_copy(name, d):
         if unit(name)[3] == 0:
             src, to = g(name, "S").at[slot_y(d)], at_y(d)
         else:
             src, to = g(name, "S").at[mod(x + d, 4)], at_x(d)
-        return rcopy(src, g(name, "R2").at[d - 1], g(name, "s").at[3 + d], g(name, "r").at[3 + d], to)
+        return rcopy(src, g(name, "R2").at[d - 1], g(name, "s").at[d - 1], g(name, "r").at[6 + d], to)
 
     def spread_x(name, d, place):
-        o = g(name, "O")
-        view = o.at[:, place] if unit(name)[3] == 0 else o.at[yhi, place]
-        return rcopy(view, view, g(name, "s").at[6 + d], g(name, "r").at[6 + d], at_x(d))
+        view = g(name, "O").at[yhi, place]
+        return rcopy(view, view, g(name, "s").at[d - 1], g(name, "r").at[9 + d], at_x(d))
+
+    def ring_x(name):
+        return Ring(name, lambda a, h: g(name, "O").at[h, a], x, at_x, 10)
 
     def spread_y(name, place):
         o = g(name, "O")
         view = o.at[place, x] if unit(name)[3] == 0 else o.at[place]
-        return rcopy(view, view, g(name, "s").at[10], g(name, "r").at[10], at_y(2))
+        return rcopy(view, view, g(name, "s").at[6], g(name, "r").at[16], at_y(2))
 
     def core_send(name):
         core_copy(name, 1 - k).start()
@@ -570,17 +623,27 @@
             return carry
 
         lax.fori_loop(0, 16, add, 0)
-        for d in (1, 3, 2):
-            first_copy(name, d).start()
+        for n in (0, 1, 2, 4):
+            first_copy(name, n).start()
+
+    def stage_pass(name):
+        mid = g(name, "T")
+        for n, e, h, last in ((0, 1, 0, 3), (1, 3, 1, 5)):
+            first_copy(name, n).wait_recv()
+            view = first_view(name, e, h)
+            view[...] = (view[...].astype(F32) + mid[h].astype(F32)).astype(BF)
+            first_copy(name, last).start()
 
     def stage_two(name):
-        for d in (1, 3, 2):
-            first_copy(name, d).wait()
+        for n in (2, 4, 3, 5):
+            first_copy(name, n).wait_recv()
+        for n in range(6):
+            first_copy(name, n).wait_send()
         w, got, total = g(name, "W"), g(name, "R1"), g(name, "S")
 
         def add(i, carry):
             mine = w[k, i, x] if unit(name)[3] == 0 else w[k, slot_y(0), i]
-            total[i] = (mine.astype(F32) + got[0, i].astype(F32) + got[1, i].astype(F32) + got[2, i].astype(F32)).astype(BF)
+            total[i] = (mine.astype(F32) + got[0, i].astype(F32) + got[1, i].astype(F32)).astype(BF)
             return carry
 
         lax.fori_loop(0, 4, add, 0)
@@ -611,11 +674,14 @@
     def stage_four(name):
         if unit(name)[3] == 0:
             take_y(name)
-            for d in (1, 3, 2):
-                spread_x(name, d, x).start()
+            ring_start(ring_x(name))
         else:
             take_x(name)
             spread_y(name, yhi).start()
+
+    def stage_four_pass(name):
+        if unit(name)[3] == 0:
+            ring_pass(ring_x(name))
 
     def results(name, core):
         o = g(name, "O")
@@ -632,32 +698,32 @@
 
     def stage_five(name):
         if unit(name)[3] == 0:
-            take_x(name)
+            for d in (1, 3, 2):
+                ring_take(ring_x(name), d)
+            ring_end(ring_x(name))
         else:
             take_y(name)
         for n, (src, dst) in enumerate(results(name, k)):
             pltpu.make_async_copy(src, dst, g(name, "l").at[n]).start()
-            rcopy(src, dst, g(name, "s").at[11 + n], g(name, "r").at[11 + n], mate).start()
+            rcopy(src, dst, g(name, "s").at[n], g(name, "r").at[17 + n], mate).start()
 
     def stage_six(name):
         for n, (src, dst) in enumerate(results(name, k)):
             pltpu.make_async_copy(src, dst, g(name, "l").at[n]).wait()
-            rcopy(src, dst, g(name, "s").at[11 + n], g(name, "r").at[11 + n], mate).wait_send()
+            rcopy(src, dst, g(name, "s").at[n], g(name, "r").at[17 + n], mate).wait_send()
         for n, (src, dst) in enumerate(results(name, 1 - k)):
-            rcopy(src, dst, g(name, "s").at[11 + n], g(name, "r").at[11 + n], mate).wait_recv()
+            rcopy(src, dst, g(name, "s").at[n], g(name, "r").at[17 + n], mate).wait_recv()
 
     def features(ref, a, core):
         at = pl.multiple_of(a * HALF + core * W, W)
         return ref[:, :, pl.ds(at, W)].reshape(4 * T, W)
 
     def grad_down(core):
-        def step(a, carry):
-            full = dot_tn(q.A[...].reshape(4 * T, H), features(q.COT, a, core)).astype(BF).reshape(2, 4, 144, W)
-            q.dn0_W[core, pl.ds(2 * a, 2)] = full[:, :, :, :128]
-            q.dn1_W[core, pl.ds(2 * a, 2)] = full[:, :, :, 128:]
-            return carry
-
-        lax.fori_loop(0, 2, step, 0)
+        both = jnp.concatenate([features(q.COT, a, core) for a in (0, 1)], axis=1)
+        full = dot_tn(q.A[...].reshape(4 * T, H), both).astype(BF).reshape(2, 4, 144, 2 * W)
+        for a in (0, 1):
+            q.dn0_W[core, 2 * a : 2 * a + 2] = full[:, :, :, a * W : a * W + 128]
+            q.dn1_W[core, 2 * a : 2 * a + 2] = full[:, :, :, a * W + 128 : (a + 1) * W]
 
     def grad_gate_up(core):
         def step(a, carry):
@@ -680,23 +746,50 @@
 
         lax.fori_loop(0, 2, step, 0)
 
+    def out_pair(pair):
+        put_pair("RF", q.OWNF, pair, dot(two_chunks(q.A, pair), q.DNW[...]))
+
+    for d in (1, 3, 2):
+        ring_take(COT, d)
+    for at, n in COLS:
+        ga = dot_nt(q.COT[...].reshape(4 * T, D), q.DNW[at : at + n, :]).reshape(4, T, n)
+        for first in (0, H):
+            lanes = slice(first + at, first + at + n)
+            q.GG[:, :, lanes] = (ga * q.GG[:, :, lanes].astype(F32)).astype(BF)
+
+    def back_pair(pair):
+        gate = dot_nt(two_chunks(q.GG, pair, slice(0, H)), q.GUW[0].reshape(D, H))
+        up = dot_nt(two_chunks(q.GG, pair, slice(H, 2 * H)), q.GUW[1].reshape(D, H))
+        put_pair("R2", q.OWN, pair, gate + up)
+
+    grad_gate_up(1 - k)
+    core_send("gt")
+    core_send("up")
+    back_pair((2, 0))
+    grad_gate_up(k)
+    stage_one("gt")
+    stage_one("up")
+    back_pair((1, 3))
+    out_pair((2, 0))
+    for ring in (XF, GF, COT):
+        ring_end(ring)
+    grad_down(1 - k)
+    core_send("dn0")
+    core_send("dn1")
+    stage_pass("gt")
+    stage_pass("up")
+    grad_down(k)
+    stage_one("dn0")
+    stage_one("dn1")
+
     def norm_back(value, scale, gain, grad):
         weighted = grad * gain
         inner = jnp.sum(weighted * value, axis=1, keepdims=True)
         back = scale * weighted - value * (scale * scale * scale) * inner / D
         return back, jnp.sum(grad * value * scale, axis=0, keepdims=True)
 
-    grad_down(1 - k)
-    core_send("dn0")
-    core_send("dn1")
-    grad_gate_up(1 - k)
-    core_send("gt")
-    core_send("up")
-    grad_down(k)
-    stage_one("dn0")
-    stage_one("dn1")
     grad_normed = reduce_sum("R2", q.OWN)
-    hidden = q.HID[...]
+    hidden = q.HID[c]
     back, grad_gain = norm_back(hidden, norm_scale(hidden), q.GA[1:2, :], grad_normed)
     q.SM[...] = jnp.zeros((8, D), F32)
     q.SM[1:2, :] = grad_gain
@@ -712,11 +805,51 @@
 
     for d in (1, 3, 2):
         gated_copy(d, c).start()
-    gather_start("GB")
+    ring_start(GB)
     q.GGR[c] = q.GGS[c]
-    grad_gate_up(k)
-    stage_one("gt")
-    stage_one("up")
+    stage_two("gt")
+    stage_two("up")
+    stage_pass("dn0")
+    stage_pass("dn1")
+
+    def home(n):
+        buf, out = ((q.MIXB, q.o_mixed), (q.GTB, q.o_gt))[n]
+        base = 6 + 2 * n
+        halves = lambda a: buf.at[:, pl.ds(pl.multiple_of(a * HALF, HALF), HALF)]
+        rows = lambda j: out.at[pl.ds(j * T, T), :]
+        near_local = pltpu.make_async_copy(halves(r), rows(k), q.sw_r.at[base])
+        near_far = rcopy(halves(r), rows(k), q.sw_s.at[base], q.sw_r.at[base + 1], mate)
+        away = rcopy(halves(1 - r), rows(k), q.sw_s.at[base + 1], q.sw_r.at[base + k], dev(r_=1 - r, k_=r))
+        return halves, rows, base, near_local, near_far, away
+
+    def home_start(n):
+        halves, rows, base, near_local, near_far, away = home(n)
+
+        @pl.when(same)
+        def _():
+            near_local.start()
+
+        @pl.when(other)
+        def _():
+            near_far.start()
+
+        away.start()
+
+    def home_wait(n):
+        halves, rows, base, near_local, near_far, away = home(n)
+
+        @pl.when(same)
+        def _():
+            near_local.wait()
+            rcopy(halves(r), rows(1 - k), q.sw_s.at[base], q.sw_r.at[base + 1], mate).wait_recv()
+
+        @pl.when(other)
+        def _():
+            near_far.wait_send()
+            for j in (0, 1):
+                rcopy(halves(r), rows(j), q.sw_s.at[base], q.sw_r.at[base + j], dev(r_=1 - r)).wait_recv()
+
+        away.wait_send()
 
     @pl.when(k == 1)
     def _():
@@ -741,13 +874,13 @@
     halo_b = rcopy(q.FM.at[:, 1:5, 0:8], q.FM.at[:, pl.ds(k, 4), pl.ds(T, 8)], q.halo.at[2], q.halo.at[3], mate)
     halo_bt = rcopy(q.FM.at[:, 1:5, 0:8], q.FM.at[:, pl.ds(1 - k, 4), pl.ds(T, 8)], q.halo.at[2], q.halo.at[3], mate)
     halo_b.start()
-    gather_pass("GB")
+    stage_two("dn0")
+    stage_two("dn1")
+    ring_pass(GB)
     halo_b.wait_send()
     halo_bt.wait_recv()
 
-    def product_back_step(i, carry):
-        e = far_first(i)
-        s = mod(c + e, 4)
+    def product_back_step(s, carry):
         grad_conv = q.GCONV[s]
         grad_product = q.ck[0:1, :] * grad_conv
         grad_product = grad_product + q.ck[1:2, :] * q.FM[0, s + 1, pl.ds(1, T)]
@@ -757,132 +890,160 @@
         q.SM[4:5, 0:W] += jnp.sum(q.FM[1, s + 1, pl.ds(0, T)] * q.PR[s, pl.ds(6, T)], axis=0, keepdims=True)
         q.GM[s, :, 0:W] = (grad_product * q.VAL[s]).astype(BF)
         q.GM[s, :, 2 * W :] = (grad_product * q.GBV[s]).astype(BF)
-        part = dot_nt(q.GM[s, :, 0:W], q.INW[0]) + dot_nt(q.GM[s, :, W : 2 * W], q.INW[1]) + dot_nt(q.GM[s, :, 2 * W :], q.INW[2])
-        put_part("R3", q.OWNF, e, part)
         return carry
 
     lax.fori_loop(0, 4, product_back_step, 0)
+
+    def in_pair(pair):
+        part = [dot_nt(two_chunks(q.GM, pair, slice(n * W, (n + 1) * W)), q.INW[n]) for n in range(3)]
+        put_pair("R3", q.OWNB, pair, part[0] + part[1] + part[2])
+
+    class Small:
+        def __init__(self, name):
+            self.name = name
+            self.own, self.other = getattr(q, name), getattr(q, name + "C")
+            self.axes = [(getattr(q, name + axis), me, at) for axis, me, at in (("X", x, at_x), ("Y", y, at_y), ("Z", c, at_z))]
+            self.sends, self.takes = getattr(q, name + "_s"), getattr(q, name + "_r")
+
+        def core(self):
+            return rcopy(self.own, self.other, self.sends.at[9], self.takes.at[9], mate)
+
+        def copy(self, n, d, a):
+            buf, _, to = self.axes[n]
+            return rcopy(buf.at[a], buf.at[a], self.sends.at[3 * n + d - 1], self.takes.at[3 * n + d - 1], to(d))
+
+        def take(self, n):
+            buf, me, _ = self.axes[n]
+            for d in (1, 2, 3):
+                self.copy(n, d, me).wait_send()
+                self.copy(n, d, mod(me - d, 4)).wait_recv()
+            return (buf[0] + buf[1]) + (buf[2] + buf[3])
+
+        def step(self, n):
+            if n == 0:
+                self.core().wait()
+                value = self.own[...] + self.other[...]
+            else:
+                value = self.take(n - 1)
+            self.own[...] = value
+            buf, me, _ = self.axes[n]
+            buf[me] = value
+            for d in (1, 2, 3):
+                self.copy(n, d, me).start()
+
+    early, late = Small("SE"), Small("SL")
+    for n in range(8):
+        q.SE[n : n + 1, :] = q.SM[1:2, n * 128 : (n + 1) * 128]
+    for n in range(8):
+        q.SE[8 + n : 9 + n, :] = q.SM[2 + n // 2 : 3 + n // 2, (n % 2) * 128 : (n % 2 + 1) * 128]
+    early.core().start()
+    in_pair((2, 0))
+    stage_three("gt")
+    stage_three("up")
+    in_pair((1, 3))
+    early.step(0)
     for d in (1, 3, 2):
-        gather_take("GB", d)
+        ring_take(GB, d)
     grad_out_in(1 - k)
     core_send("oi0")
     core_send("oi1")
+    stage_four("gt")
+    stage_four("up")
     grad_out_in(k)
-    gather_end("GB")
-    stage_two("dn0")
-    stage_two("dn1")
+    ring_end(GB)
     stage_one("oi0")
     stage_one("oi1")
-
-    grad_normed = reduce_sum("R3", q.OWNF)
-
-    def ffn_out_step(i, carry):
-        e = far_first(i)
-        s = mod(c + e, 4)
-        put_part("RF", q.OWNF, e, dot(q.A[s], q.DNW[...]))
-        return carry
-
-    def home(n):
-        buf, out = ((q.MIXB, q.o_mixed), (q.GTB, q.o_gt))[n]
-        base = 6 + 2 * n
-        halves = lambda a: buf.at[:, pl.ds(pl.multiple_of(a * HALF, HALF), HALF)]
-        rows = lambda j: out.at[pl.ds(j * T, T), :]
-        near_local = pltpu.make_async_copy(halves(r), rows(k), q.sw_r.at[base])
-        near_far = rcopy(halves(r), rows(k), q.sw_s.at[base], q.sw_r.at[base + 1], mate)
-        away = rcopy(halves(1 - r), rows(k), q.sw_s.at[base + 1], q.sw_r.at[base + k], dev(r_=1 - r, k_=r))
-        return halves, rows, base, near_local, near_far, away
-
-    def home_start(n):
-        halves, rows, base, near_local, near_far, away = home(n)
-
-        @pl.when(same)
-        def _():
-            near_local.start()
-
-        @pl.when(other)
-        def _():
-            near_far.start()
-
-        away.start()
-
-    def home_wait(n):
-        halves, rows, base, near_local, near_far, away = home(n)
-
-        @pl.when(same)
-        def _():
-            near_local.wait()
-            rcopy(halves(r), rows(1 - k), q.sw_s.at[base], q.sw_r.at[base + 1], mate).wait_recv()
-
-        @pl.when(other)
-        def _():
-            near_far.wait_send()
-            for j in (0, 1):
-                rcopy(halves(r), rows(j), q.sw_s.at[base], q.sw_r.at[base + j], dev(r_=1 - r)).wait_recv()
-
-        away.wait_send()
-
+    early.step(1)
+    out_pair((1, 3))
+    stage_three("dn0")
+    stage_three("dn1")
+    stage_pass("oi0")
+    stage_pass("oi1")
+    stage_four_pass("gt")
+    early.step(2)
+    stage_four("dn0")
+    stage_four("dn1")
+    grad_normed = reduce_sum("R3", q.OWNB)
     inputs = q.XF[c].astype(F32)
     back, grad_gain = norm_back(inputs, norm_scale(inputs), q.GA[0:1, :], grad_normed)
-    q.SM[0:1, :] = grad_gain
+    for n in range(8):
+        q.SL[n : n + 1, :] = grad_gain[:, n * 128 : (n + 1) * 128]
+    late.core().start()
     q.GTB[...] = (q.OWN[...] + back).astype(BF)
     home_start(1)
-
-    small_core = rcopy(q.SM, q.SMC, q.SM_s.at[0], q.SM_r.at[0], mate)
-    small_core.start()
-    lax.fori_loop(0, 4, ffn_out_step, 0)
-    stage_two("gt")
-    stage_two("up")
-    stage_three("dn0")
-    stage_three("dn1")
-    small_core.wait()
-
-    def small_step(buf, me, base, target, value, rows):
-        buf[me] = value
-        for d in (1, 2, 3):
-            rcopy(buf.at[me], buf.at[me], q.SM_s.at[base + d - 1], q.SM_r.at[base + d - 1], target(d)).start()
-
-    def small_take(buf, me, base, target):
-        for d in (1, 2, 3):
-            rcopy(buf.at[me], buf.at[me], q.SM_s.at[base + d - 1], q.SM_r.at[base + d - 1], target(d)).wait_send()
-            src = mod(me - d, 4)
-            rcopy(buf.at[src], buf.at[src], q.SM_s.at[base + d - 1], q.SM_r.at[base + d - 1], target(d)).wait_recv()
-        return (buf[0] + buf[1]) + (buf[2] + buf[3])
-
-    small_step(q.SMX, x, 1, at_x, q.SM[...] + q.SMC[...], 8)
     stage_two("oi0")
     stage_two("oi1")
-    stage_three("gt")
-    stage_three("up")
-    stage_four("dn0")
-    stage_four("dn1")
-    total = small_take(q.SMX, x, 1, at_x)
-    small_step(q.SMY, y, 4, at_y, total, 8)
-    q.MIXB[...] = (q.HID[...] + reduce_sum("RF", q.OWNF)).astype(BF)
-    home_start(0)
-    stage_four("gt")
-    stage_four("up")
+    late.step(0)
+    stage_five("gt")
+    stage_five("up")
+    stage_four_pass("dn0")
+    late.step(1)
     stage_three("oi0")
     stage_three("oi1")
-    total = small_take(q.SMY, y, 4, at_y)
-    small_step(q.SMZ, c, 7, at_z, total, 8)
+    q.MIXB[...] = (q.HID[c] + reduce_sum("RF", q.OWNF)).astype(BF)
+    home_start(0)
+    late.step(2)
     stage_five("dn0")
     stage_five("dn1")
     stage_four("oi0")
     stage_four("oi1")
-    stage_five("gt")
-    stage_five("up")
-    q.o_small[...] = total
-    total = small_take(q.SMZ, c, 7, at_z)
-    q.o_small[0:2, :] = total[0:2, :]
+    stage_four_pass("oi0")
+    early_gain = early.take(2)
+    late_gain = late.take(2)
+    q.SL[...] = late_gain
+    q.SEC[0:8, :] = early_gain[0:8, :]
+    q.o_small[...] = jnp.zeros((8, HALF), F32)
+    for n in range(4):
+        lanes = slice(n * 128, (n + 1) * 128)
+        q.o_small[0:1, lanes] = q.SL[pl.ds(r * 4 + n, 1), :]
+        q.o_small[1:2, lanes] = q.SEC[pl.ds(r * 4 + n, 1), :]
+    for n in range(6):
+        q.o_small[2 + n // 2 : 3 + n // 2, (n % 2) * 128 : (n % 2 + 1) * 128] = q.SE[8 + n : 9 + n, :]
     stage_five("oi0")
     stage_five("oi1")
     home_wait(0)
     home_wait(1)
     gain_send.wait_send()
-    for w in (0, 2, 3):
+    for w in (0, 3):
         weight_end(w)
     for name in ("dn0", "dn1", "gt", "up", "oi0", "oi1"):
         stage_six(name)
+
+
+def cast_kernel(mixed, tokens, small, g_in, g_out, g_gu, g_dn, o_mixed, o_tokens, o_mixer, o_kernel, o_ffn, o_in, o_out, o_gu, o_dn):
+    o_mixed[...] = mixed[...]
+    o_mixer[...] = small[0:1, :]
+    o_ffn[...] = small[1:2, :]
+    o_kernel[...] = small[2:5, 0:W]
+    for src, dst in ((tokens, o_tokens), (g_in, o_in), (g_out, o_out), (g_gu, o_gu), (g_dn, o_dn)):
+        dst[...] = src[...].astype(F32)
+
+
+def cast_all(*arrays):
+    steps = 8
+
+    def cut(shape):
+        at = len(shape) - 2
+        block = shape[:at] + (shape[at] // steps, shape[-1])
+        return pl.BlockSpec(block, lambda i: (0,) * at + (i, 0))
+
+    def whole(shape):
+        return pl.BlockSpec(shape, lambda i: (0, 0))
+
+    specs = [whole(a.shape) if n == 2 else cut(a.shape) for n, a in enumerate(arrays)]
+    small = [(1, HALF), (3, W), (1, HALF)]
+    kinds = [BF] + [F32] * 5
+    big = [cut(a.shape) for n, a in enumerate(arrays) if n != 2]
+    shapes = [jax.ShapeDtypeStruct(a.shape, kind) for a, kind in zip([a for n, a in enumerate(arrays) if n != 2], kinds)]
+    return pl.pallas_call(
+        cast_kernel,
+        grid=(steps,),
+        in_specs=specs,
+        out_specs=big[:2] + [whole(n) for n in small] + big[2:],
+        out_shape=shapes[:2] + [jax.ShapeDtypeStruct(n, F32) for n in small] + shapes[2:],
+        compiler_params=pltpu.CompilerParams(vmem_limit_bytes=60 * 2**20),
+        name="cast_all",
+    )(*arrays)
 
 
 def per_device(
@@ -897,8 +1058,6 @@
     conv_reach,
     cotangent,
 ):
-    reach = jnp.broadcast_to(conv_reach.astype(BF).reshape(2, 2, T, 1), (2, 2, T, 128))
-    gains = jnp.concatenate([mixer_gain[None], ffn_gain[None], jnp.zeros((6, HALF), F32)], axis=0)
     hbm = pl.BlockSpec(memory_space=pl.ANY)
     vmem = pl.BlockSpec(memory_space=pltpu.VMEM)
     mixed, grad_tokens, small, g_in, g_out, g_gu, g_dn = pl.pallas_call(
@@ -906,32 +1065,42 @@
         out_shape=(
             jax.ShapeDtypeStruct((2 * T, HALF), BF),
             jax.ShapeDtypeStruct((2 * T, HALF), BF),
-            jax.ShapeDtypeStruct((8, D), F32),
+            jax.ShapeDtypeStruct((8, HALF), F32),
             jax.ShapeDtypeStruct((3, 2, 2, 4, 32, W), BF),
             jax.ShapeDtypeStruct((2, 4, 32, HALF), BF),
             jax.ShapeDtypeStruct((2, 2, 2, 4, 32, H), BF),
             jax.ShapeDtypeStruct((2, 4, 144, HALF), BF),
         ),
-        in_specs=[hbm, hbm, hbm, hbm, vmem, hbm, hbm, hbm, hbm],
+        in_specs=[hbm, hbm, vmem, vmem, vmem, vmem, hbm, hbm, hbm, hbm],
         out_specs=(hbm, hbm, vmem, hbm, hbm, hbm, hbm),
         scratch_shapes=list(scratch_list().values()),
         compiler_params=pltpu.CompilerParams(
             collective_id=0, has_side_effects=True, vmem_limit_bytes=60 * 2**20
         ),
         name="block_step",
-    )(tokens, cotangent, reach, gains, conv_kernel, in_weight, out_weight, gate_up_weight, down_weight)
-    mine = lax.dynamic_slice_in_dim(small, lax.axis_index("row") * HALF, HALF, axis=1)
-    return (
+    )(
+        tokens,
+        cotangent,
+        conv_reach.reshape(4, T),
+        mixer_gain.reshape(1, HALF),
+        ffn_gain.reshape(1, HALF),
+        conv_kernel,
+        in_weight,
+        out_weight,
+        gate_up_weight.reshape(2, 4, 2, 64, H),
+        down_weight,
+    )
+    results = cast_all(
         mixed,
-        grad_tokens.astype(F32),
-        mine[0],
-        g_in.reshape(3, HALF, W).astype(F32),
-        small[2:5, :W],
-        g_out.reshape(W, HALF).astype(F32),
-        mine[1],
-        g_gu.reshape(2, HALF, H).astype(F32),
-        g_dn.reshape(H, HALF).astype(F32),
+        grad_tokens,
+        small,
+        g_in.reshape(3, HALF, W),
+        g_out.reshape(W, HALF),
+        g_gu.reshape(2, HALF, H),
+        g_dn.reshape(H, HALF),
     )
+    mixed, grad_tokens, mixer, kernel_grad, ffn, g_in, g_out, g_gu, g_dn = results
+    return (mixed, grad_tokens, mixer.reshape(HALF), g_in, kernel_grad, g_out, ffn.reshape(HALF), g_gu, g_dn)
 
 
 def solution(mesh):

time: 156 us -> 142 us (0.910)
  other arithmetic: 11.2 us -> 0 us
  local copies, waits for them, and re-layouts: 4.34 us -> 0 us
    convert_element_type x6 -> x0, other arithmetic: 9.8 us -> none  [the longest x1 4.25 us: per_device(): g_gu.reshape(2, HALF, H).astype(F32)]
    pallas_call x0 -> x1, Pallas kernels: none -> 8.12 us  [cast_all(): pl.pallas_call(cast_kernel, grid=(steps,), in_specs=specs, out_specs=big[...]
    pallas_call x1, Pallas kernels: 140 us -> 133 us  [per_device(): pl.pallas_call(kernel, out_shape=(jax.ShapeDtypeStruct((2 * T, HALF), BF)...]
    slice x2 -> x0, local copies, waits for them, and re-layouts: 2.74 us -> none  [the longest x1 1.45 us: per_device(): mine[1]]
where the time goes in v3:
time: 142 us
  Pallas kernels  141 us (99%)
    pallas_call x1, Pallas kernels, per_device(): pl.pallas_call(kernel, out_shape=(jax.ShapeDtypeStruct((2 * T, HALF), BF)...  133 us
    pallas_call x1, Pallas kernels, cast_all(): pl.pallas_call(cast_kernel, grid=(steps,), in_specs=specs, out_specs=big[...  8.12 us

profile of v3, /device:TPU:1, one launch (start us, length us, event | category | flops | bytes accessed | tf_op | source)
XLA Modules:
  0.0 142.0 jit_solution(10022609530925047478)
XLA Ops:
  0.6 133.1 %block_step.1 = (bf16[256,512]{1,0:T(8,128)(2,1)}, bf16[256,512]{1,0:T(8,128)(2,1)}, f32[8,512]{1,0:T(8,128)}, bf16[3,2,2,4,32,256]{5,4,3,2,1,0:T(8,128)(2,1)}, ...) custom-call(bf16[256,512]{1,0:T(8,128)(2,1)} %refs_0_.1, ...), custom_call_target="tpu_custom_call" | custom-call | tf_op jit(solution)/shard_map/block_step/pallas_call | solution.py:1063
  133.7 8.1 %cast_all.1 = (bf16[256,512]{1,0:T(8,128)(2,1)}, f32[256,512]{1,0:T(8,128)}, f32[1,512]{1,0:T(1,128)}, f32[3,256]{1,0:T(4,128)}, f32[1,512]{1,0:T(1,128)}, /*ind...) custom-call(bf16[256,512]{1,0:T(8,128)(2,1)} %get-tuple-element.25.mixed, ...), custom_call_target="tpu_custom_call" | custom-call | tf_op jit(solution)/shard_map/cast_all/pallas_call | solution.py:1038

commit v4 on v3

--- a/solution.py
+++ b/solution.py
@@ -336,8 +336,6 @@
     gain_send.start()
     out_local.start()
     out_row(r).start()
-    weight_start(0)
-    swap_start(1)
 
     class Ring:
         def __init__(self, name, view, me, target, first=0):
@@ -415,25 +413,29 @@
             send[1] = part.astype(BF)
             reduce_copy(name, 0).start()
             reduce_copy(name, 1).start()
-        elif e == 1:
-            send[0, HT:T] = part[HT:].astype(BF)
-            reduce_copy(name, 2).start()
-            reduce_copy(name, 0).wait_recv()
-            send[0, 0:HT] = (part[:HT] + mid[0].astype(F32)).astype(BF)
-            reduce_copy(name, 3).start()
-        else:
-            send[2, 0:HT] = part[:HT].astype(BF)
-            reduce_copy(name, 4).start()
-            reduce_copy(name, 1).wait_recv()
-            send[2, HT:T] = (part[HT:] + mid[1].astype(F32)).astype(BF)
-            reduce_copy(name, 5).start()
+
+    def put_last(name, before, after):
+        mid, send = getattr(q, name + "_T"), getattr(q, name + "_B")
+        send[0, HT:T] = before[HT:].astype(BF)
+        reduce_copy(name, 2).start()
+        send[2, 0:HT] = after[:HT].astype(BF)
+        reduce_copy(name, 4).start()
+        reduce_copy(name, 0).wait_recv()
+        send[0, 0:HT] = (before[:HT] + mid[0].astype(F32)).astype(BF)
+        reduce_copy(name, 3).start()
+        reduce_copy(name, 1).wait_recv()
+        send[2, HT:T] = (after[HT:] + mid[1].astype(F32)).astype(BF)
+        reduce_copy(name, 5).start()
 
     def two_chunks(ref, pair, lanes=slice(None)):
         return jnp.concatenate([ref[mod(c + e, 4), :, lanes] for e in pair], axis=0)
 
     def put_pair(name, own, pair, part):
-        for n, e in enumerate(pair):
-            put_part(name, own, e, part[n * T : (n + 1) * T])
+        if pair == (1, 3):
+            put_last(name, part[:T], part[T:])
+        else:
+            for n, e in enumerate(pair):
+                put_part(name, own, e, part[n * T : (n + 1) * T])
 
     def arrival(i):
         return i + lax.div(i, 2) - 2 * lax.div(i, 3)
@@ -443,17 +445,18 @@
 
     swap_wait(0)
     ring_start(XF)
-    for n in (0, 1):
-        gu_row(n, r).start()
-    swap_start(2)
+    weight_start(0)
     out_local.wait()
     out_row(1 - r).wait_recv()
     for d in (1, 3, 2):
         out_col(d, c).start()
-    weight_start(3)
     gain_local.wait()
     gain_take.wait_recv()
     weight_forward(0)
+    for n in (0, 1):
+        gu_row(n, r).start()
+    swap_start(1)
+    swap_start(2)
     weight_ready(0)
 
     @pl.when(k == 0)
@@ -466,20 +469,20 @@
         @pl.when(i == 1)
         def _():
             ring_pass(XF)
-            ring_take(XF, 1)
-
-        @pl.when(i == 2)
-        def _():
             for d in (1, 3, 2):
                 out_col(d, mod(c - d, 4)).wait_recv()
             ring_start(OUX)
+            ring_take(XF, 1)
+
+        @pl.when(i == 2)
+        def _():
             ring_take(XF, 3)
-
-        @pl.when(i == 3)
-        def _():
             for n in (0, 1):
                 gu_row(n, 1 - r).wait_recv()
             ring_start(GUX)
+
+        @pl.when(i == 3)
+        def _():
             ring_take(XF, 2)
 
         inputs = q.XF[s].astype(F32)
@@ -497,6 +500,9 @@
     halo_f = rcopy(q.PR.at[0:4, pl.ds(T, 8)], q.PR.at[pl.ds(k, 4), 0:8], q.halo.at[0], q.halo.at[1], mate)
     halo_ft = rcopy(q.PR.at[0:4, pl.ds(T, 8)], q.PR.at[pl.ds(1 - k, 4), 0:8], q.halo.at[0], q.halo.at[1], mate)
     halo_f.start()
+    weight_start(3)
+    swap_wait(2)
+    ring_start(COT, (0, 1))
     swap_wait(1)
     halo_f.wait_send()
     halo_ft.wait_recv()
@@ -523,8 +529,7 @@
     ring_pass(OUX)
     ring_pass(GUX)
     ring_pass(GF)
-    swap_wait(2)
-    ring_start(COT)
+    ring_start(COT, (2, 3))
     for d in (1, 3, 2):
         ring_take(OUX, d)
     out_core(k).start()
@@ -734,17 +739,21 @@
 
         lax.fori_loop(0, 2, step, 0)
 
-    def grad_out_in(core):
+    def grad_in(core):
         def step(a, carry):
             rows = features(q.N1, a, core)
-            gated = q.GF[c]
-            q.oi0_W[core, pl.ds(2 * a, 2), :, :, 0:W] = dot_tn(gated, features(q.GB, a, core)).astype(BF).reshape(2, 4, 32, W)
             into = dot_tn(rows, q.GM[...].reshape(4 * T, 3 * W)).astype(BF).reshape(2, 4, 32, 3 * W)
             q.oi0_W[core, pl.ds(2 * a, 2), :, :, W:] = into[:, :, :, 0:W]
             q.oi1_W[core, pl.ds(2 * a, 2)] = into[:, :, :, W:]
             return carry
 
         lax.fori_loop(0, 2, step, 0)
+
+    def grad_out(core):
+        both = jnp.concatenate([features(q.GB, a, core) for a in (0, 1)], axis=1)
+        full = dot_tn(q.GF[c], both).astype(BF).reshape(2, 4, 32, 2 * W)
+        for a in (0, 1):
+            q.oi0_W[core, 2 * a : 2 * a + 2, :, :, 0:W] = full[:, :, :, a * W : (a + 1) * W]
 
     def out_pair(pair):
         put_pair("RF", q.OWNF, pair, dot(two_chunks(q.A, pair), q.DNW[...]))
@@ -762,22 +771,20 @@
         up = dot_nt(two_chunks(q.GG, pair, slice(H, 2 * H)), q.GUW[1].reshape(D, H))
         put_pair("R2", q.OWN, pair, gate + up)
 
+    back_pair((2, 0))
     grad_gate_up(1 - k)
     core_send("gt")
     core_send("up")
-    back_pair((2, 0))
+    back_pair((1, 3))
     grad_gate_up(k)
     stage_one("gt")
     stage_one("up")
-    back_pair((1, 3))
     out_pair((2, 0))
     for ring in (XF, GF, COT):
         ring_end(ring)
     grad_down(1 - k)
     core_send("dn0")
     core_send("dn1")
-    stage_pass("gt")
-    stage_pass("up")
     grad_down(k)
     stage_one("dn0")
     stage_one("dn1")
@@ -805,12 +812,9 @@
 
     for d in (1, 3, 2):
         gated_copy(d, c).start()
-    ring_start(GB)
     q.GGR[c] = q.GGS[c]
-    stage_two("gt")
-    stage_two("up")
-    stage_pass("dn0")
-    stage_pass("dn1")
+    stage_pass("gt")
+    stage_pass("up")
 
     def home(n):
         buf, out = ((q.MIXB, q.o_mixed), (q.GTB, q.o_gt))[n]
@@ -859,6 +863,7 @@
     for d in (1, 3, 2):
         gated_copy(d, c).wait_send()
         gated_copy(d, mod(c - d, 4)).wait_recv()
+    ring_start(GB)
 
     def conv_back_step(s, carry):
         grad_gated = q.GGR[s].astype(F32)
@@ -874,9 +879,8 @@
     halo_b = rcopy(q.FM.at[:, 1:5, 0:8], q.FM.at[:, pl.ds(k, 4), pl.ds(T, 8)], q.halo.at[2], q.halo.at[3], mate)
     halo_bt = rcopy(q.FM.at[:, 1:5, 0:8], q.FM.at[:, pl.ds(1 - k, 4), pl.ds(T, 8)], q.halo.at[2], q.halo.at[3], mate)
     halo_b.start()
-    stage_two("dn0")
-    stage_two("dn1")
-    ring_pass(GB)
+    stage_pass("dn0")
+    stage_pass("dn1")
     halo_b.wait_send()
     halo_bt.wait_recv()
 
@@ -937,32 +941,36 @@
     for n in range(8):
         q.SE[8 + n : 9 + n, :] = q.SM[2 + n // 2 : 3 + n // 2, (n % 2) * 128 : (n % 2 + 1) * 128]
     early.core().start()
+    ring_pass(GB)
+    stage_two("gt")
+    stage_two("up")
+    grad_in(1 - k)
+    core_send("oi1")
     in_pair((2, 0))
+    stage_two("dn0")
+    stage_two("dn1")
+    grad_in(k)
+    stage_one("oi1")
+    for d in (1, 3, 2):
+        ring_take(GB, d)
+    grad_out(1 - k)
+    core_send("oi0")
+    in_pair((1, 3))
     stage_three("gt")
     stage_three("up")
-    in_pair((1, 3))
+    grad_out(k)
+    stage_one("oi0")
+    ring_end(GB)
     early.step(0)
-    for d in (1, 3, 2):
-        ring_take(GB, d)
-    grad_out_in(1 - k)
-    core_send("oi0")
-    core_send("oi1")
-    stage_four("gt")
-    stage_four("up")
-    grad_out_in(k)
-    ring_end(GB)
-    stage_one("oi0")
-    stage_one("oi1")
-    early.step(1)
+    stage_pass("oi1")
     out_pair((1, 3))
     stage_three("dn0")
     stage_three("dn1")
+    stage_four("gt")
+    stage_four("up")
     stage_pass("oi0")
-    stage_pass("oi1")
-    stage_four_pass("gt")
-    early.step(2)
-    stage_four("dn0")
-    stage_four("dn1")
+    early.step(1)
+    stage_two("oi1")
     grad_normed = reduce_sum("R3", q.OWNB)
     inputs = q.XF[c].astype(F32)
     back, grad_gain = norm_back(inputs, norm_scale(inputs), q.GA[0:1, :], grad_normed)
@@ -972,22 +980,25 @@
     q.GTB[...] = (q.OWN[...] + back).astype(BF)
     home_start(1)
     stage_two("oi0")
-    stage_two("oi1")
+    stage_four_pass("gt")
+    stage_four("dn0")
+    stage_four("dn1")
+    stage_three("oi1")
+    stage_three("oi0")
     late.step(0)
+    early.step(2)
+    stage_four_pass("dn0")
+    stage_four("oi1")
+    stage_four("oi0")
+    late.step(1)
     stage_five("gt")
     stage_five("up")
-    stage_four_pass("dn0")
-    late.step(1)
-    stage_three("oi0")
-    stage_three("oi1")
+    stage_four_pass("oi0")
+    late.step(2)
     q.MIXB[...] = (q.HID[c] + reduce_sum("RF", q.OWNF)).astype(BF)
     home_start(0)
-    late.step(2)
     stage_five("dn0")
     stage_five("dn1")
-    stage_four("oi0")
-    stage_four("oi1")
-    stage_four_pass("oi0")
     early_gain = early.take(2)
     late_gain = late.take(2)
     q.SL[...] = late_gain
@@ -1020,7 +1031,7 @@
 
 
 def cast_all(*arrays):
-    steps = 8
+    steps = 4
 
     def cut(shape):
         at = len(shape) - 2

time: 142 us -> 138 us (0.972)
  Pallas kernels: 141 us -> 137 us
    pallas_call x1, Pallas kernels: 133 us -> 130 us  [per_device(): pl.pallas_call(kernel, out_shape=(jax.ShapeDtypeStruct((2 * T, HALF), BF)...]
where the time goes in v4:
time: 138 us; the launch traced here: 137 us
  Pallas kernels  137 us (99%)
    pallas_call x1, Pallas kernels, per_device(): pl.pallas_call(kernel, out_shape=(jax.ShapeDtypeStruct((2 * T, HALF), BF)...  130 us
    pallas_call x1, Pallas kernels, cast_all(): pl.pallas_call(cast_kernel, grid=(steps,), in_specs=specs, out_specs=big[...  6.72 us

profile of v4, /device:TPU:1, one launch (start us, length us, event | category | flops | bytes accessed | tf_op | source)
XLA Modules:
  0.0 137.4 jit_solution(6907714046233011337)
XLA Ops:
  0.6 129.9 %block_step.1 = (bf16[256,512]{1,0:T(8,128)(2,1)}, bf16[256,512]{1,0:T(8,128)(2,1)}, f32[8,512]{1,0:T(8,128)}, bf16[3,2,2,4,32,256]{5,4,3,2,1,0:T(8,128)(2,1)}, ...) custom-call(bf16[256,512]{1,0:T(8,128)(2,1)} %refs_0_.1, ...), custom_call_target="tpu_custom_call" | custom-call | tf_op jit(solution)/shard_map/block_step/pallas_call | solution.py:1074
  130.6 6.7 %cast_all.1 = (bf16[256,512]{1,0:T(8,128)(2,1)}, f32[256,512]{1,0:T(8,128)}, f32[1,512]{1,0:T(1,128)}, f32[3,256]{1,0:T(4,128)}, f32[1,512]{1,0:T(1,128)}, /*ind...) custom-call(bf16[256,512]{1,0:T(8,128)(2,1)} %get-tuple-element.25.mixed, ...), custom_call_target="tpu_custom_call" | custom-call | tf_op jit(solution)/shard_map/cast_all/pallas_call | solution.py:1049
